TPU v7x, 256 devices: a whole 4x4x8 slice. The times are simulated.
256 devices in a mesh: rep: 32 (over y, z_hi, x), tp: 8 (over z_lo, core).
Axes of the slice: x: 4, y: 4, z: 8 (z_hi: 2, z_lo: 4; z = z_hi * 4 + z_lo), core: 2. Of those that a mesh axis runs over, the one named last changes fastest.
Arguments:
- queries: bfloat16 [1024, 4096], P('rep', 'tp'), may hold values from -150 to 150
- k_cache: bfloat16 [1024, 128, 1024], P('rep', None, 'tp'), may hold values from -6.5 to 6.5
- v_cache: bfloat16 [1024, 128, 1024], P('rep', None, 'tp'), may hold values from -24 to 24
- new_keys: bfloat16 [1024, 1024], P('rep', 'tp'), may hold values from -6 to 6
- new_values: bfloat16 [1024, 1024], P('rep', 'tp'), may hold values from -24 to 24
- kv_len: int32 [1024], P('rep'), may hold values from 2 to 127
- send_rows: int32 [32, 8], P('rep'), may hold values from -1 to 31, as said below
- recv_rows: int32 [32, 8], P('rep'), may hold values from -1 to 31, as said below
- out_weight: bfloat16 [8192, 4096], P(None, 'tp'), may hold values from -0.09375 to 0.09375
- adapter_down: bfloat16 [256, 64, 4096], P('rep', None, 'tp'), may hold values from -0.09375 to 0.09375
- adapter_up: bfloat16 [256, 64, 8192], P('rep', None, 'tp'), may hold values from -0.75 to 0.75
- sectioned_down: bfloat16 [32, 64, 4096], P('rep', None, 'tp'), may hold values from -0.09375 to 0.09375
- sectioned_up: bfloat16 [32, 64, 8192], P('rep', None, 'tp'), may hold values from -0.75 to 0.75
- install: int32 [32, 8], P('rep'), may hold values from -1 to 31
- adapter_slot: int32 [1024], P('rep'), may hold values from 0 to 7
Outputs:
- mixed: bfloat16 [1024, 8192], P('rep', 'tp')
Inputs may be any that keep to these rules, and one draw needn't show every extreme that they name: `send_rows`: column j of a replica's row names a request that moves to the replica that many places after it (wrapping): 1 place for j // 2 = 0, else (j // 2 + 1) * 4 places; the named requests of one row are distinct; at most 2 requests go from one replica to another, and some replica receives exactly 2 from each of the 4 replicas that send to it. recv_rows[d, j] >= 0 exactly where the column j entry of the replica that column's distance before d in send_rows is >= 0; the named rows of one replica are distinct.
All inputs are finite; a program needn't handle non-finite values.
Results may differ from a plain program's by a relative error of at most 0.02.
Values may be sent and summed in bfloat16 or wider, within the bound.
A program may use at most 64 MiB of HBM per device.

v0:
```python
import jax
import jax.numpy as jnp
from jax import lax
from jax.sharding import PartitionSpec as P

HD = 128
ADAPTER_RANK = 64
RESIDENT_SLOTS = 8
SPAN = 4
CAP = 2


def attend_rows(queries, keys, values, new_key, new_value, lengths):
    requests = queries.shape[0]
    positions = keys.shape[1]
    heads = new_key.shape[1] // HD
    groups = queries.shape[1] // (heads * HD)
    query = queries.reshape(requests, heads, groups, HD)
    key_rows = keys.reshape(requests, positions, heads, HD)
    value_rows = values.reshape(requests, positions, heads, HD)
    scale = HD ** (-0.5)
    scores = (
        jnp.einsum("rkgd,rlkd->rkgl", query, key_rows, preferred_element_type=jnp.float32) * scale
    )
    live = jnp.arange(positions)[None, :] < lengths[:, None]
    scores = jnp.where(live[:, None, None, :], scores, -jnp.inf)
    own = (
        jnp.einsum(
            "rkgd,rkd->rkg",
            query,
            new_key.reshape(requests, heads, HD),
            preferred_element_type=jnp.float32,
        )
        * scale
    )
    top = jnp.maximum(jnp.max(scores, axis=-1), own)
    weights = jnp.exp(scores - top[..., None])
    own_weight = jnp.exp(own - top)
    total = jnp.sum(weights, axis=-1) + own_weight
    own_b = lax.optimization_barrier(own_weight.astype(jnp.bfloat16)).astype(jnp.float32)
    summed = jnp.einsum(
        "rkgl,rlkd->rkgd",
        weights.astype(jnp.bfloat16),
        value_rows,
        preferred_element_type=jnp.float32,
    )
    own_value = new_value.astype(jnp.float32).reshape(requests, heads, HD)
    summed = summed + own_b[..., None] * own_value[:, :, None, :]
    return (summed / total[..., None]).astype(jnp.bfloat16).reshape(requests, heads * groups * HD)


def pick_rows(k_cache, v_cache, length_b, chosen):
    present = chosen >= 0
    rows = jnp.maximum(chosen, 0)
    keys_out = jnp.where(present[:, None, None], k_cache[rows], jnp.zeros((), jnp.bfloat16))
    values_out = jnp.where(present[:, None, None], v_cache[rows], jnp.zeros((), jnp.bfloat16))
    length_out = jnp.where(present, length_b[rows], jnp.zeros((), jnp.bfloat16))
    return (keys_out, values_out, length_out)


def body(
    queries,
    k_cache,
    v_cache,
    new_keys,
    new_values,
    kv_len,
    send_rows,
    recv_rows,
    out_weight,
    adapter_down,
    adapter_up,
    sectioned_down,
    sectioned_up,
    install,
    adapter_slot,
):
    replicas = lax.axis_size("rep")
    stride = replicas // (2 * SPAN)
    me = lax.axis_index("rep")
    requests = queries.shape[0]
    width = SPAN * CAP
    column = jnp.arange(width, dtype=jnp.int32)
    send_here = send_rows[0]
    recv_here = recv_rows[0]
    length_b = kv_len.astype(jnp.bfloat16)
    dest = jnp.arange(replicas, dtype=jnp.int32)
    offset = (dest - me) % replicas
    far = offset // stride
    far_ok = (offset % stride == 0) & (far >= 2) & (far <= SPAN)
    group = jnp.where(offset == 1, 1, jnp.where(far_ok, far, 0))
    usable = group >= 1
    entry = (
        jnp.clip(group - 1, 0, SPAN - 1)[:, None] * CAP + jnp.arange(CAP, dtype=jnp.int32)[None, :]
    )
    chosen = jnp.where(usable[:, None], send_here[entry], -1).reshape(-1)
    keys_out, values_out, length_out = pick_rows(k_cache, v_cache, length_b, chosen)
    got_keys, got_values, got_length = (
        lax.all_to_all(keys_out, "rep", split_axis=0, concat_axis=0, tiled=True),
        lax.all_to_all(values_out, "rep", split_axis=0, concat_axis=0, tiled=True),
        lax.all_to_all(length_out, "rep", split_axis=0, concat_axis=0, tiled=True),
    )
    col_group = column // CAP
    distance_col = jnp.where(col_group == 0, 1, (col_group + 1) * stride)
    source = (me - distance_col) % replicas
    flat = source * CAP + column % CAP
    arrive_keys = got_keys[flat]
    arrive_values = got_values[flat]
    arrive_length = got_length[flat]
    match = recv_here[None, :] == jnp.arange(requests, dtype=jnp.int32)[:, None]
    takes = jnp.any(match, axis=1)
    which = jnp.sum(jnp.where(match, column[None, :], 0), axis=1)
    keys = jnp.where(takes[:, None, None], arrive_keys[which], k_cache)
    values = jnp.where(takes[:, None, None], arrive_values[which], v_cache)
    lengths = jnp.where(takes, arrive_length[which].astype(jnp.int32), kv_len)
    gathered_down, gathered_up = (
        lax.all_gather(sectioned_down, "rep", axis=0, tiled=True),
        lax.all_gather(sectioned_up, "rep", axis=0, tiled=True),
    )
    picks = install[0]
    keep_old = (picks < 0)[:, None, None]
    down = jnp.where(keep_old, adapter_down, gathered_down[jnp.maximum(picks, 0)])
    up = jnp.where(keep_old, adapter_up, gathered_up[jnp.maximum(picks, 0)])
    attn = attend_rows(queries, keys, values, new_keys, new_values, lengths)
    onehot = (adapter_slot[:, None] == jnp.arange(RESIDENT_SLOTS, dtype=jnp.int32)[None, :]).astype(
        jnp.float32
    )
    partial_value = jnp.einsum("rq,skq->rsk", attn, down, preferred_element_type=jnp.float32)
    partial_value = (partial_value * onehot[:, :, None]).reshape(
        requests, RESIDENT_SLOTS * ADAPTER_RANK
    )
    columns = out_weight.shape[0] // lax.axis_size("tp")
    up_flat = up.reshape(RESIDENT_SLOTS * ADAPTER_RANK, columns)
    down_projected = lax.psum(partial_value.astype(jnp.bfloat16), "tp")
    base_output = lax.psum_scatter(
        lax.dot_general(
            out_weight, attn, (((1,), (1,)), ((), ())), preferred_element_type=jnp.float32
        ).astype(jnp.bfloat16),
        "tp",
        scatter_dimension=0,
        tiled=True,
    ).astype(jnp.float32)
    low_rank_delta = lax.dot_general(
        up_flat, down_projected, (((0,), (1,)), ((), ())), preferred_element_type=jnp.float32
    )
    return (base_output + low_rank_delta).T.astype(jnp.bfloat16)


def solution(mesh):
    placed = (
        P("rep", "tp"),
        P("rep", None, "tp"),
        P("rep", None, "tp"),
        P("rep", "tp"),
        P("rep", "tp"),
        P("rep"),
        P("rep", None),
        P("rep", None),
        P(None, "tp"),
        P("rep", None, "tp"),
        P("rep", None, "tp"),
        P("rep", None, "tp"),
        P("rep", None, "tp"),
        P("rep", None),
        P("rep"),
    )
    return jax.shard_map(
        body, mesh=mesh, in_specs=placed, out_specs=P("rep", "tp"), check_vma=False
    )
```

profile of v0, /device:TPU:1, one launch (start us, length us, event | category | flops | bytes accessed | tf_op | source)
XLA Modules:
  0.0 269.4 jit_solution(15433222379273873612)
XLA Ops:
  7.4 0.7 all-gather.5.cloned.1.call-update
  8.4 0.8 gather_fusion
  9.6 0.8 gather_fusion.1
  10.6 0.6 copy.27
  11.2 14.5 %all-to-all-start = ((bf16[32,2,1]{1,2,0:T(2,128)(2,1)}), bf16[32,2,1]{1,2,0:T(2,128)(2,1)S(1)}, u32[]{:S(2)}, u32[]{:S(2)}) async-start(bf16[32,2,1]{1,2,0:T(2,128)(2,1)} %copy.27), calls=%async_computation | async-start | bytes 32768 | tf_op jit(solution)/shard_map/all_to_all | solution.py:101
  25.7 1.0 gather_fusion.4
  26.7 3.4 %gather_fusion.7 = bf16[64,128,128]{2,1,0:T(8,128)(2,1)} fusion(bf16[32,128,128]{2,1,0:T(8,128)(2,1)} %param.17, s32[1024]{0:T(1024)S(1)} %pad_clamp_fusion.3), kind=kCustom, calls=%fused_computation.7 | custom fusion | bytes 4194560 | tf_op jit(solution)/shard_map/gather | solution.py:56
  30.3 4.1 %broadcast_select_fusion.1 = (bf16[64,128,128]{2,1,0:T(8,128)(2,1)}, bf16[64,128,128]{2,1,0:T(8,128)(2,1)}) fusion(bf16[64,128,128]{2,1,0:T(8,128)(2,1)S(1)} %gather_fusion.4, pred[64]{0:T(512)(128)(4,1)S(1)} %ge.41, bf16[64,128,128]{2,1,0:T(8,128)(2,1)} %gather_fusion.7), kind=kLoop, calls=%fused_computation.15 | loop fusion | flops 2097152 | bytes 8388672 | tf_op jit(solution)/shard_map/jit(_where)/select_n | solution.py:55
  34.4 2.3 all-to-all-done
  36.7 9.3 %all-to-all-start.1 = ((bf16[64,128,128]{2,1,0:T(8,128)(2,1)}), bf16[64,128,128]{2,1,0:T(8,128)(2,1)S(1)}, u32[]{:S(2)}, u32[]{:S(2)}) async-start(bf16[64,128,128]{2,1,0:T(8,128)(2,1)} %get-tuple-element.7), calls=%async_computation.1 | async-start | bytes 4194304 | tf_op jit(solution)/shard_map/all_to_all | solution.py:99
  46.1 0.7 all-gather.3.cloned.1.call-update
  46.8 37.8 %all-to-all-done.1 = bf16[64,128,128]{2,1,0:T(8,128)(2,1)S(1)} async-done(((bf16[64,128,128]{2,1,0:T(8,128)(2,1)}), bf16[64,128,128]{2,1,0:T(8,128)(2,1)S(1)}, u32[]{:S(2)}, u32[]{:S(2)}) %all-to-all-start.1) | async-done | bytes 2097184 | tf_op jit(solution)/shard_map/all_to_all | solution.py:99
  84.6 1.3 copy-done.4
  85.9 4.6 %all-to-all-start.2 = ((bf16[64,128,128]{2,1,0:T(8,128)(2,1)}), bf16[64,128,128]{2,1,0:T(8,128)(2,1)S(1)}, u32[]{:S(2)}, u32[]{:S(2)}) async-start(bf16[64,128,128]{2,1,0:T(8,128)(2,1)} %get-tuple-element.8), calls=%async_computation.2 | async-start | bytes 4194304 | tf_op jit(solution)/shard_map/all_to_all | solution.py:100
  90.6 0.6 convert_element_type.57
  91.5 0.5 maximum_bitcast_fusion
  92.3 0.6 gather_fusion.2
  93.0 0.7 gather_fusion.3
  93.8 2.2 gather_fusion.5
  96.0 1.7 gather_fusion.6
  97.7 2.0 fusion.34
  100.2 34.0 %all-to-all-done.2 = bf16[64,128,128]{2,1,0:T(8,128)(2,1)S(1)} async-done(((bf16[64,128,128]{2,1,0:T(8,128)(2,1)}), bf16[64,128,128]{2,1,0:T(8,128)(2,1)S(1)}, u32[]{:S(2)}, u32[]{:S(2)}) %all-to-all-start.2) | async-done | bytes 2097184 | tf_op jit(solution)/shard_map/all_to_all | solution.py:100
  134.2 0.6 gather_fusion.8
  134.8 0.7 gather_fusion.9
  135.6 0.5 fusion.7
  136.1 6.8 %fusion = bf16[8192,32]{0,1:T(8,128)(2,1)} fusion(bf16[8192,512]{1,0:T(8,128)(2,1)} %param.23, bf16[4,8,4,128]{3,2,1,0:T(4,128)(2,1)S(1)} %bitcast.41), kind=kOutput, calls=%fused_computation.13 | convolution fusion | flops 268697600 | bytes 8945664 | tf_op jit(solution)/shard_map/dot_general | solution.py:136
  143.0 2.3 gather_fusion.11
  145.3 0.4 fusion.2
  145.9 54.3 %psum.7 = bf16[32,512]{1,0:T(8,128)(2,1)S(1)} all-reduce(bf16[32,512]{1,0:T(8,128)(2,1)S(1)} %convert_element_type.64), channel_id=1, replica_groups=mesh['rep'=32,'tp'=8] {'tp'}, use_global_device_ids=true, to_apply=%region_5.6 | all-reduce | flops 16384 | bytes 65536 | tf_op jit(solution)/shard_map/psum | solution.py:134
  200.2 56.9 %all-gather.3.cloned.1.call-done = bf16[32,64,1024]{2,1,0:T(8,128)(2,1)} async-done(((bf16[1,64,1024]{2,1,0:T(8,128)(2,1)}), bf16[32,64,1024]{2,1,0:T(8,128)(2,1)}) %all-gather.3.cloned.1.call-update) | async-done | bytes 4194320 | tf_op jit(solution)/shard_map/all_gather | solution.py:118
  257.1 2.8 %gather_fusion.10 = bf16[8,64,1024]{2,1,0:T(8,128)(2,1)S(1)} fusion(bf16[32,64,1024]{2,1,0:T(8,128)(2,1)} %all-gather.3.cloned.1.call-done, s32[1024]{0:T(1024)S(1)} %pad_clamp_fusion), kind=kCustom, calls=%fused_computation.10 | custom fusion | bytes 2097184 | tf_op jit(solution)/shard_map/gather | solution.py:123
  260.2 1.8 fusion.3
  (81 shorter events, 2.6 us)
Async XLA Ops:
  7.4 84.6 %copy-start = (bf16[32,128]{1,0:T(8,128)(2,1)S(1)}, bf16[32,128]{1,0:T(8,128)(2,1)}, u32[]{:S(2)}) copy-start(bf16[32,128]{1,0:T(8,128)(2,1)} %param.18) | copy-start | bytes 24580
  7.4 1.0 copy-start.1
  7.4 135.6 %all-gather.5.cloned.1.call-start = ((), (), s32[]{:S(2)}) async-start(), calls=%async_computation.6 | async-start | bytes 2162688 | tf_op jit(solution)/shard_map/all_gather | solution.py:117
  8.3 1.2 copy-start.11
  8.3 17.4 %copy-start.2 = (bf16[32,128,128]{2,1,0:T(8,128)(2,1)S(1)}, bf16[32,128,128]{2,1,0:T(8,128)(2,1)}, u32[]{:S(2)}) copy-start(bf16[32,128,128]{2,1,0:T(8,128)(2,1)} %param.16) | copy-start | bytes 3145732
  11.2 25.5 %all-to-all-start = ((bf16[32,2,1]{1,2,0:T(2,128)(2,1)}), bf16[32,2,1]{1,2,0:T(2,128)(2,1)S(1)}, u32[]{:S(2)}, u32[]{:S(2)}) async-start(bf16[32,2,1]{1,2,0:T(2,128)(2,1)} %copy.27), calls=%async_computation | async-start | bytes 32768 | tf_op jit(solution)/shard_map/all_to_all | solution.py:101
  36.7 47.9 %all-to-all-start.1 = ((bf16[64,128,128]{2,1,0:T(8,128)(2,1)}), bf16[64,128,128]{2,1,0:T(8,128)(2,1)S(1)}, u32[]{:S(2)}, u32[]{:S(2)}) async-start(bf16[64,128,128]{2,1,0:T(8,128)(2,1)} %get-tuple-element.7), calls=%async_computation.1 | async-start | bytes 4194304 | tf_op jit(solution)/shard_map/all_to_all | solution.py:99
  46.0 211.1 %all-gather.3.cloned.1.call-start = ((), (), s32[]{:S(2)}) async-start(), calls=%async_computation.5 | async-start | bytes 4325376 | tf_op jit(solution)/shard_map/all_gather | solution.py:118
  84.6 1.4 copy-start.4
  84.6 6.0 %copy-start.6 = (bf16[32,512]{1,0:T(8,128)(2,1)S(1)}, bf16[32,512]{1,0:T(8,128)(2,1)}, u32[]{:S(2)}) copy-start(bf16[32,512]{1,0:T(8,128)(2,1)} %param.15) | copy-start | bytes 98308
  84.6 6.0 %copy-start.8 = (bf16[32,128]{1,0:T(8,128)(2,1)S(1)}, bf16[32,128]{1,0:T(8,128)(2,1)}, u32[]{:S(2)}) copy-start(bf16[32,128]{1,0:T(8,128)(2,1)} %param.19) | copy-start | bytes 24580
  84.6 6.7 %copy-start.15 = (s32[1,8]{1,0:T(1,128)S(1)}, s32[1,8]{1,0:T(1,128)}, u32[]{:S(2)}) copy-start(s32[1,8]{1,0:T(1,128)} %param.22) | copy-start | bytes 100
  84.6 6.9 %copy-start.16 = (s32[1,8]{1,0:T(1,128)S(1)}, s32[1,8]{1,0:T(1,128)}, u32[]{:S(2)}) copy-start(s32[1,8]{1,0:T(1,128)} %param.28) | copy-start | bytes 100
  85.9 48.3 %all-to-all-start.2 = ((bf16[64,128,128]{2,1,0:T(8,128)(2,1)}), bf16[64,128,128]{2,1,0:T(8,128)(2,1)S(1)}, u32[]{:S(2)}, u32[]{:S(2)}) async-start(bf16[64,128,128]{2,1,0:T(8,128)(2,1)} %get-tuple-element.8), calls=%async_computation.2 | async-start | bytes 4194304 | tf_op jit(solution)/shard_map/all_to_all | solution.py:100
  90.5 169.7 %reduce-scatter.2.cloned.1.call-start = ((), (), s32[]{:S(2)}) async-start(), calls=%async_computation.4 | async-start | bytes 589824 | tf_op jit(solution)/shard_map/reduce_scatter | solution.py:135
  91.5 8.3 %copy-start.12 = (pred[32]{0:T(512)(128)(4,1)}, pred[32]{0:T(512)(128)(4,1)S(1)}, u32[]{:S(2)}) copy-start(pred[32]{0:T(512)(128)(4,1)S(1)} %fusion.25) | copy-start | bytes 100
  99.8 35.8 %copy-start.3 = (bf16[32,128,128]{2,1,0:T(8,128)(2,1)S(1)}, bf16[32,128,128]{2,1,0:T(8,128)(2,1)}, u32[]{:S(2)}) copy-start(bf16[32,128,128]{2,1,0:T(8,128)(2,1)} %param.17) | copy-start | bytes 3145732
  99.8 35.8 %copy-start.7 = (f32[32,128]{1,0:T(8,128)S(1)}, f32[32,128]{1,0:T(8,128)}, u32[]{:S(2)}) copy-start(f32[32,128]{1,0:T(8,128)} %convert_element_type.57) | copy-start | bytes 49156
  134.8 0.8 copy-start.13
  136.1 6.8 %copy-start.10 = (s32[8]{0:T(128)S(1)}, s32[8]{0:T(128)}, u32[]{:S(2)}) copy-start(s32[8]{0:T(128)} %maximum_bitcast_fusion) | copy-start | bytes 100
  136.1 6.9 %copy-start.17 = (s32[1,8]{1,0:T(1,128)S(1)}, s32[1,8]{1,0:T(1,128)}, u32[]{:S(2)}) copy-start(s32[1,8]{1,0:T(1,128)} %param.28) | copy-start | bytes 100
  136.1 6.9 %copy-start.9 = (s32[32]{0:T(128)S(1)}, s32[32]{0:T(128)}, u32[]{:S(2)}) copy-start(s32[32]{0:T(128)} %param.29) | copy-start | bytes 388
  136.1 9.2 %copy-start.14 = (bf16[8,64,512]{2,1,0:T(8,128)(2,1)S(1)}, bf16[8,64,512]{2,1,0:T(8,128)(2,1)}, u32[]{:S(2)}) copy-start(bf16[8,64,512]{2,1,0:T(8,128)(2,1)} %param.24) | copy-start | bytes 1572868
  143.0 117.0 %copy-start.5 = (bf16[8,64,1024]{2,1,0:T(8,128)(2,1)S(1)}, bf16[8,64,1024]{2,1,0:T(8,128)(2,1)}, u32[]{:S(2)}) copy-start(bf16[8,64,1024]{2,1,0:T(8,128)(2,1)} %param.25) | copy-start | bytes 3145732
Sparse Core Ops, SparseCore 0:
  11.7 125.0 all-gather.4
  140.2 116.9 all-gather.2
Sparse Core Ops, SparseCore 1:
  143.0 67.7 reduce-scatter.1
where the time goes:
time: 270 us; the launch traced here: 269 us
  waiting for transfers between devices  133 us (49%)
  blocking collectives  54.3 us (20%)
  starting transfers between devices  28.5 us (11%)
  local copies, waits for them, and re-layouts  20.8 us (8%)
  between operations  15.3 us (6%)
  matrix products  11.6 us (4%)
  other arithmetic  6.36 us (2%)
    all_gather x1, waiting for transfers between devices, body(): lax.all_gather(sectioned_up, 'rep', axis=0, tiled=True)  56.9 us
    psum x1, blocking collectives, body(): down_projected = lax.psum(partial_value.astype(jnp.bfloat16), 'tp')  54.3 us
    all_to_all x1, waiting for transfers between devices, body(): lax.all_to_all(keys_out, 'rep', split_axis=0, concat_axis=0, tiled=True)  37.8 us
    all_to_all x1, waiting for transfers between devices, body(): lax.all_to_all(values_out, 'rep', split_axis=0, concat_axis=0, tiled=True)  34 us
    all_to_all x1, starting transfers between devices, body(): lax.all_to_all(length_out, 'rep', split_axis=0, concat_axis=0, tiled=True)  14.5 us
    all_to_all x1, starting transfers between devices, body(): lax.all_to_all(keys_out, 'rep', split_axis=0, concat_axis=0, tiled=True)  9.33 us
    dot_general x1, matrix products, body(): lax.dot_general(out_weight, attn, (((1,), (1,)), ((), ())), preferred_ele...  6.78 us
  transfers between devices with their start and end apart: 6, of which 4 were waited for; matrix products, arithmetic and copies ran while one was open for 13% of the time, Pallas kernels for 0%

commit v1 on v0

v1 whole, which is shorter than its diff:
```python
import functools

import jax
import jax.numpy as jnp
from jax import lax
from jax.experimental import pallas as pl
from jax.experimental.pallas import tpu as pltpu
from jax.sharding import PartitionSpec as P

MESH = pl.DeviceIdType.MESH
F32 = jnp.float32
BF16 = jnp.bfloat16

HD = 128
HEADS = 4
REQ = 32
LMAX = 128
RANK = 64
SLOTS = 8
SPAN = 4
CAP = 2
REP = 32
TP = 8
ROW = 4
QW = HEADS * HD
OUT = 1024
RANK_PART = RANK // ROW
OUT_PART = OUT // ROW
SCALE = HD**-0.5
DISTANCES = (1, 8, 12, 16)


def iota(shape, dim):
    return lax.broadcasted_iota(jnp.int32, shape, dim)


def dot(a, b):
    return lax.dot_general(a, b, (((1,), (0,)), ((), ())), preferred_element_type=F32)


def dot_nt(a, b):
    return lax.dot_general(a, b, (((1,), (1,)), ((), ())), preferred_element_type=F32)


def remote(src, dst, ssem, rsem, device):
    return pltpu.make_async_remote_copy(
        src_ref=src,
        dst_ref=dst,
        send_sem=ssem,
        recv_sem=rsem,
        device_id=device,
        device_id_type=MESH,
    )


def softmax_parts(scores, own, live):
    scores = jnp.where(live, scores * SCALE, -jnp.inf)
    own = own * SCALE
    top = jnp.maximum(jnp.max(scores, axis=1, keepdims=True), own)
    weights = jnp.exp(scores - top)
    own_weight = jnp.exp(own - top)
    total = jnp.sum(weights, axis=1, keepdims=True) + own_weight
    return weights.astype(BF16), own_weight.astype(BF16).astype(F32), total


def to_column(row, rows):
    spread = jnp.where(iota((rows, 128), 0) == iota((rows, 128), 1), row, 0)
    return jnp.sum(spread.astype(F32), axis=1, keepdims=True).astype(jnp.int32)


def kernel(
    q_ref,
    k_hbm,
    v_hbm,
    nk_ref,
    nv_ref,
    len_row,
    slot_row,
    len_s,
    send_s,
    recv_s,
    install_s,
    w_hbm,
    adown_hbm,
    aup_hbm,
    sdown_hbm,
    sup_hbm,
    out_ref,
    kbuf,
    vbuf,
    wbuf,
    adown,
    aup,
    sdn,
    sup,
    qout,
    qin,
    meta,
    res,
    mig,
    loc,
    merged,
    obuf,
    fold,
    perm,
    msg,
    msg_sib,
    bc,
    sexp,
    dlt_out,
    dlt_in,
    sib_out,
    sib_in,
    rs_own,
    rs_out,
    rs_in,
    load_sem,
    s1_local,
    s1_ssem,
    s1_rsem,
    s2_ssem,
    s2_rsem,
    q_ssem,
    q_rsem,
    meta_ssem,
    meta_rsem,
    mig_ssem,
    mig_rsem,
    loc_ssem,
    loc_rsem,
    msg_sem,
    bc_ssem,
    bc_rsem,
    dlt_ssem,
    dlt_rsem,
    sib_ssem,
    sib_rsem,
    rs_ssem,
    rs_rsem,
):
    r = lax.axis_index("rep")
    t = lax.axis_index("tp")
    x = r % 4
    zh = (r // 4) % 2
    y = r // 8
    row0 = r - x
    z = t // 2
    core = t % 2
    sib = (r, t + 1 - 2 * core)

    barrier = pltpu.get_barrier_semaphore()

    def greet_rep(i, carry):
        pl.semaphore_signal(
            barrier, inc=1, device_id=((r + i) % REP, t), device_id_type=MESH
        )
        return carry

    lax.fori_loop(1, REP, greet_rep, 0)

    def greet_row(i, carry):
        peer = (row0 + (x + i // 3) % 4, ((z + 1 + i % 3) % 4) * 2 + core)
        pl.semaphore_signal(barrier, inc=1, device_id=peer, device_id_type=MESH)
        return carry

    lax.fori_loop(0, 12, greet_row, 0)
    pl.semaphore_signal(barrier, inc=1, device_id=sib, device_id_type=MESH)

    k_load = pltpu.make_async_copy(k_hbm, kbuf, load_sem.at[0])
    v_load = pltpu.make_async_copy(v_hbm, vbuf, load_sem.at[1])
    ad_load = pltpu.make_async_copy(adown_hbm, adown, load_sem.at[2])
    w_load = pltpu.make_async_copy(w_hbm, wbuf, load_sem.at[3])
    au_load = pltpu.make_async_copy(aup_hbm, aup, load_sem.at[4])
    for copy in (k_load, v_load, ad_load, w_load, au_load):
        copy.start()

    queries = q_ref[...]
    q_heads = jnp.concatenate(
        [queries[:, h * HD : (h + 1) * HD] for h in range(HEADS)], axis=0
    )
    new_keys = nk_ref[...]
    new_values = nv_ref[...]
    stacked = jnp.concatenate([q_heads, new_keys, new_values], axis=0)
    line = iota((64, 192), 0)
    place = line % 16
    col = iota((64, 192), 1)
    kind = jnp.where(
        place < 8,
        place % 4,
        jnp.where(place < 10, 4, jnp.where(place < 12, 5, 9)),
    )
    within = jnp.where(place < 8, place // 4, place % 2)
    entry = (line // 16) * CAP + within
    wanted = jnp.full((64, 192), -1, jnp.int32)
    for j in range(SPAN * CAP):
        wanted = jnp.where(entry == j, recv_s[0, j], wanted)
    pick = (kind == col // REQ) & (wanted == col % REQ)
    gathered = dot(pick.astype(BF16), stacked).astype(BF16)
    for g in range(SPAN):
        qout[g] = gathered[g * 16 : (g + 1) * 16]

    lane1 = iota((1, 128), 1)
    recv4 = jnp.full((1, 128), -1, jnp.int32)
    for j in range(SPAN * CAP):
        recv4 = jnp.where(lane1 // 4 == j, recv_s[0, j], recv4)
    slots = slot_row[...]
    target = jnp.full((1, REQ), -1, jnp.int32)
    for k in range(SLOTS):
        target = jnp.where(slots == k, install_s[0, k], target)
    target = jnp.concatenate([target, jnp.full((1, 128 - REQ), -1, jnp.int32)], axis=1)
    sub8 = iota((8, 128), 0)
    meta[x] = jnp.where(sub8 == 0, recv4, jnp.where(sub8 == 1, target, -1))

    pl.semaphore_wait(barrier, 31 + 12 + 1)

    sends = []

    q_copies = []
    for g, distance in enumerate(DISTANCES):
        copy = remote(
            qout.at[g],
            qin.at[g],
            q_ssem.at[g],
            q_rsem.at[g],
            ((r + REP - distance) % REP, t),
        )
        copy.start()
        q_copies.append(copy)
    sends += q_copies

    my_dn = pl.ds(pl.multiple_of(r * RANK_PART, RANK_PART), RANK_PART)
    my_up = pl.ds(pl.multiple_of(r * RANK, RANK), RANK)

    def dn_part(c):
        return sdown_hbm.at[pl.ds(pl.multiple_of(c * RANK_PART, RANK_PART), RANK_PART)]

    def up_part(c):
        return sup_hbm.at[:, pl.ds(pl.multiple_of(c * OUT_PART, OUT_PART), OUT_PART)]

    own_dn = pltpu.make_async_copy(dn_part(x), sdn.at[my_dn], s1_local.at[0])
    own_up = pltpu.make_async_copy(up_part(x), sup.at[my_up], s1_local.at[1])
    own_dn.start()
    own_up.start()
    near_dn, near_up, far_dn, far_up = [], [], [], []
    for o in range(1, 4):
        c = (x + o) % 4
        near_dn.append(
            remote(dn_part(c), sdn.at[my_dn], s1_ssem.at[0, o], s1_rsem.at[0, o], (row0 + c, t))
        )
        near_up.append(
            remote(up_part(c), sup.at[my_up], s1_ssem.at[1, o], s1_rsem.at[1, o], (row0 + c, t))
        )
    other0 = y * 8 + (1 - zh) * 4
    for o in range(4):
        c = (x + o) % 4
        far_dn.append(
            remote(dn_part(c), sdn.at[my_dn], s1_ssem.at[2, o], s1_rsem.at[2, o], (other0 + c, t))
        )
        far_up.append(
            remote(up_part(c), sup.at[my_up], s1_ssem.at[3, o], s1_rsem.at[3, o], (other0 + c, t))
        )
    for copy in far_dn + near_dn + near_up + far_up:
        copy.start()
    sends += near_dn + near_up + far_dn + far_up

    meta_copies = []
    for o in range(1, 4):
        copy = remote(
            meta.at[x], meta.at[x], meta_ssem.at[o], meta_rsem.at[o], (row0 + (x + o) % 4, t)
        )
        copy.start()
        meta_copies.append(copy)
    sends += meta_copies

    def stage2(half, tag):
        first = y * 8 + half * 4
        dn_rows = pl.ds(pl.multiple_of(first * RANK_PART, 4 * RANK_PART), 4 * RANK_PART)
        up_rows = pl.ds(pl.multiple_of(first * RANK, 4 * RANK), 4 * RANK)
        dn, up = [], []
        for o in range(1, 4):
            peer = ((r + 8 * o) % REP, t)
            dn.append(
                remote(
                    sdn.at[dn_rows], sdn.at[dn_rows], s2_ssem.at[tag, o], s2_rsem.at[tag, o], peer
                )
            )
            up.append(
                remote(
                    sup.at[up_rows],
                    sup.at[up_rows],
                    s2_ssem.at[2 + tag, o],
                    s2_rsem.at[2 + tag, o],
                    peer,
                )
            )
        return dn, up

    s2_near_dn, s2_near_up = stage2(zh, 0)
    s2_far_dn, s2_far_up = stage2(1 - zh, 1)
    sends += s2_near_dn + s2_near_up + s2_far_dn + s2_far_up

    fc = iota((5 * 512, 128), 0)
    fl = iota((5 * 512, 128), 1)
    block = fc // 512
    goal = jnp.where(block < 4, block * RANK_PART + fc % RANK_PART, 64 + fc % RANK)
    fold[...] = (fl == goal).astype(BF16)
    pc = iota((512, 512), 0)
    pj = iota((512, 512), 1)
    inner = pc % 128
    hit = (
        (inner < 64)
        & (inner // RANK_PART == pj // 128)
        & (pj % 64 == (pc // 128) * RANK_PART + pc % RANK_PART)
    )
    perm[...] = hit.astype(BF16)

    own_dn.wait()
    k_load.wait()
    er = iota((256, 128), 0)
    ec = iota((256, 128), 1)
    spread_q = ((er % 8 == ec // REQ) & (er // 8 == ec % REQ)).astype(BF16)
    q_local = dot(spread_q, q_heads)
    spread_r = iota((256, REQ), 0) // 8 == iota((256, REQ), 1)
    new_kv = dot(spread_r.astype(BF16), jnp.concatenate([new_keys, new_values], axis=1))
    lengths = jnp.sum(
        jnp.where(spread_r, len_row[...], 0).astype(F32), axis=1, keepdims=True
    ).astype(jnp.int32)
    scores = lax.dot_general(
        q_local.reshape(REQ, 8, HD).astype(BF16),
        kbuf[...],
        (((2,), (2,)), ((0,), (0,))),
        preferred_element_type=F32,
    ).reshape(256, LMAX)
    own = jnp.sum(q_local * new_kv[:, :HD], axis=1, keepdims=True)
    weights, own_b, total = softmax_parts(scores, own, ec < lengths)
    v_load.wait()
    summed = lax.dot_general(
        weights.reshape(REQ, 8, LMAX),
        vbuf[...],
        (((2,), (1,)), ((0,), (0,))),
        preferred_element_type=F32,
    ).reshape(256, HD)
    obuf[...] = (summed + own_b * new_kv[:, HD:]) / total
    for h in range(HEADS):
        loc[x, :, h * HD : (h + 1) * HD] = obuf[pl.ds(h, REQ, stride=8), :].astype(BF16)

    loc_copies = []
    for o in range(1, 4):
        copy = remote(
            loc.at[x], loc.at[x], loc_ssem.at[o], loc_rsem.at[o], (row0 + (x + o) % 4, t)
        )
        copy.start()
        loc_copies.append(copy)
    sends += loc_copies

    for copy in q_copies:
        copy.wait_recv()
    head8 = iota((8, HD), 0) // HEADS == 0
    line32 = iota((32, 128), 0) // HEADS
    moved_len = jnp.zeros((32, 128), jnp.int32)
    moved_scores, moved_own, moved_values, places = [], [], [], []
    for g in range(SPAN):
        arrived = qin[g]
        arrived_f = arrived.astype(F32)
        q8 = arrived[0:8]
        parts = []
        for i in range(CAP):
            j = g * CAP + i
            at = jnp.maximum(send_s[0, j], 0)
            places.append(at)
            parts.append(dot_nt(q8, kbuf[at]))
            moved_len = jnp.where(line32 == j, len_s[0, at], moved_len)
        moved_scores.append(jnp.where(head8, parts[0], parts[1]))
        key = jnp.where(head8, arrived_f[8:9], arrived_f[9:10])
        moved_own.append(jnp.sum(arrived_f[0:8] * key, axis=1, keepdims=True))
        moved_values.append(jnp.where(head8, arrived_f[10:11], arrived_f[11:12]))
    m_weights, m_own, m_total = softmax_parts(
        jnp.concatenate(moved_scores, axis=0),
        jnp.concatenate(moved_own, axis=0),
        iota((32, 128), 1) < moved_len,
    )
    m_summed = []
    m_wf = m_weights.astype(F32)
    for g in range(SPAN):
        w8 = m_wf[g * 8 : (g + 1) * 8].astype(BF16)
        a = dot(w8, vbuf[places[g * CAP]])
        b = dot(w8, vbuf[places[g * CAP + 1]])
        m_summed.append(jnp.where(head8, a, b))
    m_out = (
        jnp.concatenate(m_summed, axis=0) + m_own * jnp.concatenate(moved_values, axis=0)
    ) / m_total
    m_out = m_out.astype(BF16).astype(F32)
    for g in range(SPAN):
        res[g] = m_out[g * 8 : (g + 1) * 8]

    mig_sends = []
    for g, distance in enumerate(DISTANCES):
        home = (r + distance) % REP
        home_x = home % 4
        for c in range(ROW):
            device = home - home_x + c
            dst = mig.at[home_x, pl.ds(8 * g, 8)]
            copy = remote(
                res.at[g], dst, mig_ssem.at[g, c], mig_rsem.at[home_x, g], (device, t)
            )
            if g == 0:
                here = pltpu.make_async_copy(res.at[g], dst, mig_rsem.at[home_x, g])

                @pl.when(device == r)
                def _():
                    here.start()

                @pl.when(device != r)
                def _():
                    copy.start()

                mig_sends.append((copy, device))
            else:
                copy.start()
                sends.append(copy)

    for copy in near_dn:
        copy.wait_recv()
    for copy in s2_near_dn:
        copy.start()
    for copy in far_dn:
        copy.wait_recv()
    for copy in s2_far_dn:
        copy.start()
    own_up.wait()
    for copy in near_up:
        copy.wait_recv()
    for copy in s2_near_up:
        copy.start()

    for copy in meta_copies:
        copy.wait_recv()
    for copy in loc_copies:
        copy.wait_recv()
    for h in range(ROW):
        for g in range(SPAN):
            remote(res.at[0], mig.at[h, pl.ds(8 * g, 8)], mig_ssem.at[g, 0], mig_rsem.at[h, g], sib).wait_recv()
    mh = iota((128, 32), 0)
    ml = iota((128, 32), 1)
    tcols = []
    for h in range(ROW):
        tile = meta[h]
        tcols.append(to_column(tile[1:2], REQ))
        recv_row = tile[0:1, 0:32]
        put = ((mh % REQ == recv_row) & (mh // REQ == ml % 4)).astype(BF16)
        rows = dot(put, mig[h].astype(BF16)).astype(BF16)
        taken = jnp.max(
            jnp.where(iota((REQ, 32), 0) == recv_row, 1.0, 0.0), axis=1, keepdims=True
        )
        here = loc[h]
        for k in range(HEADS):
            span = slice(k * HD, (k + 1) * HD)
            merged[h * REQ : (h + 1) * REQ, span] = jnp.where(
                taken > 0.5, rows[k * REQ : (k + 1) * REQ], here[:, span]
            )

    mine = merged[pl.ds(pl.multiple_of(x * REQ, REQ), REQ), :]

    w_load.wait()

    def project(zq, cq):
        first = pl.multiple_of((zq * 2 + cq) * OUT, OUT)
        return dot_nt(mine, wbuf[pl.ds(first, OUT), :])

    sib_copies = []
    rs_copies = []
    order = (2, 1, 3, 0)

    def opposite(n):
        zq = (z + order[n]) % 4
        sib_out[n] = project(zq, 1 - core).astype(BF16)
        copy = remote(sib_out.at[n], sib_in.at[n], sib_ssem.at[n], sib_rsem.at[n], sib)
        copy.start()
        sib_copies.append(copy)

    def same(n):
        rs_own[n] = project((z + order[n]) % 4, core)

    def pass_on(n):
        zq = (z + order[n]) % 4
        sib_copies[n].wait_recv()
        both = rs_own[n] + sib_in[n].astype(F32)
        if order[n] == 0:
            rs_own[n] = both
            return
        rs_out[n] = both.astype(BF16)
        copy = remote(
            rs_out.at[n], rs_in.at[n], rs_ssem.at[n], rs_rsem.at[n], (r, zq * 2 + core)
        )
        copy.start()
        rs_copies.append(copy)

    opposite(0)
    same(0)
    opposite(1)
    pass_on(0)
    same(1)

    ad_load.wait()
    slot_col = to_column(
        jnp.concatenate([slots, jnp.full((1, 128 - REQ), -1, jnp.int32)], axis=1), REQ
    )
    target_col = to_column(meta[x][1:2], REQ)
    resident = target_col < 0
    c512 = iota((REQ, 512), 1)
    part = dot_nt(mine, adown[...])
    pieces = [jnp.where((c512 // RANK == slot_col) & resident, part, 0.0)]
    for copy in s2_near_dn + s2_far_dn:
        copy.wait_recv()
    part = dot_nt(merged[...], sdn[...])
    sections = [
        jnp.where(c512 // RANK_PART == tcols[h], part[h * REQ : (h + 1) * REQ], 0.0)
        for h in range(ROW)
    ]
    masked = jnp.concatenate(sections + pieces, axis=1).astype(BF16)
    msg[0] = dot(masked, fold[...]).astype(BF16)
    msg_copy = remote(msg.at[0], msg_sib, msg_sem.at[0], msg_sem.at[1], sib)
    msg_copy.start()
    for copy in far_up:
        copy.wait_recv()
    for copy in s2_far_up:
        copy.start()
    opposite(2)
    pass_on(1)
    msg_copy.wait_recv()
    bc[x, z] = (msg[0].astype(F32) + msg_sib[...].astype(F32)).astype(BF16)
    bc_copies = []
    for xo in range(4):
        for zo in range(4):
            if xo == 0 and zo == 0:
                continue
            copy = remote(
                bc.at[x, z],
                bc.at[x, z],
                bc_ssem.at[xo, zo],
                bc_rsem.at[xo, zo],
                (row0 + (x + xo) % 4, ((z + zo) % 4) * 2 + core),
            )
            copy.start()
            bc_copies.append(copy)
    sends += bc_copies
    same(2)
    opposite(3)
    pass_on(2)
    same(3)
    pass_on(3)

    for copy in bc_copies:
        copy.wait_recv()
    sums = []
    for h in range(ROW):
        sums.append(
            (bc[h, 0].astype(F32) + bc[h, 1].astype(F32))
            + (bc[h, 2].astype(F32) + bc[h, 3].astype(F32))
        )
    shrunk = dot(jnp.concatenate(sums, axis=1).astype(BF16), perm[...])
    lane = iota((REQ, 128), 1)
    for h in range(ROW):
        ranks = shrunk[:, h * 128 : (h + 1) * 128]
        for n in range(16):
            sexp[h * REQ : (h + 1) * REQ, n * 128 : (n + 1) * 128] = jnp.where(
                lane // RANK + 2 * n == tcols[h], ranks, 0.0
            ).astype(BF16)
    for copy in s2_near_up + s2_far_up:
        copy.wait_recv()
    delta = dot(sexp[...], sup[...])
    dlt_copies = []
    for h in range(ROW):
        dlt_out[h] = delta[h * REQ : (h + 1) * REQ].astype(BF16)
    dlt_in[x] = dlt_out[x]
    for o in range(1, 4):
        c = (x + o) % 4
        copy = remote(
            dlt_out.at[c], dlt_in.at[x], dlt_ssem.at[o], dlt_rsem.at[o], (row0 + c, t)
        )
        copy.start()
        dlt_copies.append(copy)
    sends += dlt_copies

    au_load.wait()
    own_sum = (bc[x, 0].astype(F32) + bc[x, 1].astype(F32)) + (
        bc[x, 2].astype(F32) + bc[x, 3].astype(F32)
    )
    ranks = jnp.where(lane < RANK, pltpu.roll(own_sum, RANK, 1), own_sum)
    spread = jnp.concatenate(
        [
            jnp.where((lane // RANK + 2 * n == slot_col) & resident, ranks, 0.0)
            for n in range(SLOTS // 2)
        ],
        axis=1,
    ).astype(BF16)
    acc = dot(spread, aup[...]) + rs_own[3]

    for copy in rs_copies:
        copy.wait_recv()
    for n in range(3):
        acc = acc + rs_in[n].astype(F32)
    for copy in dlt_copies:
        copy.wait_recv()
    out_ref[...] = (
        acc + jnp.concatenate([dlt_in[h].astype(F32) for h in range(ROW)], axis=1)
    ).astype(BF16)

    msg_copy.wait_send()
    for copy in sib_copies + rs_copies + sends:
        copy.wait_send()
    for copy, device in mig_sends:

        @pl.when(device != r)
        def _():
            copy.wait_send()


def body(
    queries,
    k_cache,
    v_cache,
    new_keys,
    new_values,
    kv_len,
    send_rows,
    recv_rows,
    out_weight,
    adapter_down,
    adapter_up,
    sectioned_down,
    sectioned_up,
    install,
    adapter_slot,
):
    vmem = pl.BlockSpec(memory_space=pltpu.VMEM)
    smem = pl.BlockSpec(memory_space=pltpu.SMEM)
    hbm = pl.BlockSpec(memory_space=pl.ANY)
    dma = pltpu.SemaphoreType.DMA
    lengths = kv_len.reshape(1, REQ)
    return pl.pallas_call(
        kernel,
        out_shape=jax.ShapeDtypeStruct((REQ, OUT), BF16),
        in_specs=[vmem, hbm, hbm, vmem, vmem, vmem, vmem, smem, smem, smem, smem]
        + [hbm] * 5,
        out_specs=vmem,
        scratch_shapes=[
            pltpu.VMEM((REQ, LMAX, HD), BF16),
            pltpu.VMEM((REQ, LMAX, HD), BF16),
            pltpu.VMEM((TP * OUT, QW), BF16),
            pltpu.VMEM((SLOTS * RANK, QW), BF16),
            pltpu.VMEM((SLOTS * RANK, OUT), BF16),
            pltpu.VMEM((REP * RANK_PART, QW), BF16),
            pltpu.VMEM((REP * RANK, OUT_PART), BF16),
            pltpu.VMEM((SPAN, 16, HD), BF16),
            pltpu.VMEM((SPAN, 16, HD), BF16),
            pltpu.VMEM((ROW, 8, 128), jnp.int32),
            pltpu.VMEM((SPAN, 8, HD), F32),
            pltpu.VMEM((ROW, 32, HD), F32),
            pltpu.VMEM((ROW, REQ, QW), BF16),
            pltpu.VMEM((ROW * REQ, QW), BF16),
            pltpu.VMEM((256, HD), F32),
            pltpu.VMEM((5 * 512, 128), BF16),
            pltpu.VMEM((512, 512), BF16),
            pltpu.VMEM((1, REQ, 128), BF16),
            pltpu.VMEM((REQ, 128), BF16),
            pltpu.VMEM((4, 4, REQ, 128), BF16),
            pltpu.VMEM((ROW * REQ, REP * RANK), BF16),
            pltpu.VMEM((ROW, REQ, OUT_PART), BF16),
            pltpu.VMEM((ROW, REQ, OUT_PART), BF16),
            pltpu.VMEM((4, REQ, OUT), BF16),
            pltpu.VMEM((4, REQ, OUT), BF16),
            pltpu.VMEM((4, REQ, OUT), F32),
            pltpu.VMEM((3, REQ, OUT), BF16),
            pltpu.VMEM((3, REQ, OUT), BF16),
            dma((5,)),
            dma((2,)),
            dma((4, 4)),
            dma((4, 4)),
            dma((4, 4)),
            dma((4, 4)),
            dma((4,)),
            dma((4,)),
            dma((4,)),
            dma((4,)),
            dma((4, 4)),
            dma((4, 4)),
            dma((4,)),
            dma((4,)),
            dma((2,)),
            dma((4, 4)),
            dma((4, 4)),
            dma((4,)),
            dma((4,)),
            dma((4,)),
            dma((4,)),
            dma((4,)),
            dma((4,)),
        ],
        compiler_params=pltpu.CompilerParams(
            collective_id=0, has_side_effects=True, vmem_limit_bytes=48 << 20
        ),
    )(
        queries,
        k_cache,
        v_cache,
        new_keys,
        new_values,
        lengths,
        adapter_slot.reshape(1, REQ),
        lengths,
        send_rows,
        recv_rows,
        install,
        out_weight,
        adapter_down.reshape(SLOTS * RANK, QW),
        adapter_up.reshape(SLOTS * RANK, OUT),
        sectioned_down.reshape(RANK, QW),
        sectioned_up.reshape(RANK, OUT),
    )


def solution(mesh):
    placed = (
        P("rep", "tp"),
        P("rep", None, "tp"),
        P("rep", None, "tp"),
        P("rep", "tp"),
        P("rep", "tp"),
        P("rep"),
        P("rep", None),
        P("rep", None),
        P(None, "tp"),
        P("rep", None, "tp"),
        P("rep", None, "tp"),
        P("rep", None, "tp"),
        P("rep", None, "tp"),
        P("rep", None),
        P("rep"),
    )
    return jax.shard_map(
        body, mesh=mesh, in_specs=placed, out_specs=P("rep", "tp"), check_vma=False
    )
```

time: 270 us -> 59.8 us (0.22)
  waiting for transfers between devices: 133 us -> 0 us
  blocking collectives: 54.3 us -> 0 us
  Pallas kernels: 0 us -> 46.8 us
  starting transfers between devices: 28.5 us -> 0 us
  between operations: 15.3 us -> 0.02 us
  matrix products: 11.6 us -> 0 us
  local copies, waits for them, and re-layouts: 20.8 us -> 12.5 us
  other arithmetic: 6.36 us -> 0 us
    all_to_all x3 -> x0, waiting for transfers between devices: 74.1 us -> none  [the longest x1 37.8 us: body(): lax.all_to_all(keys_out, 'rep', split_axis=0, concat_axis=0, tiled=True)]
    all_gather x2 -> x0, waiting for transfers between devices: 57 us -> none  [the longest x1 56.9 us: body(): lax.all_gather(sectioned_up, 'rep', axis=0, tiled=True)]
    psum x1 -> x0, blocking collectives: 54.3 us -> none  [body(): down_projected = lax.psum(partial_value.astype(jnp.bfloat16), 'tp')]
    pallas_call x0 -> x1, Pallas kernels: none -> 46.8 us  [body(): pl.pallas_call(kernel, out_shape=jax.ShapeDtypeStruct((REQ, OUT), BF16),...]
    all_to_all x3 -> x0, starting transfers between devices: 28.4 us -> none  [the longest x1 14.5 us: body(): lax.all_to_all(length_out, 'rep', split_axis=0, concat_axis=0, tiled=True)]
    gather x15 -> x0, local copies, waits for them, and re-layouts: 17.9 us -> none  [the longest x1 3.41 us: pick_rows(): v_cache[rows]]
    dot_general x6 -> x0, matrix products: 11.6 us -> none  [the longest x1 6.78 us: body(): lax.dot_general(out_weight, attn, (((1,), (1,)), ((), ())), preferred_ele...]
    unnamed x36 -> x29, local copies, waits for them, and re-layouts: 1.43 us -> 12.5 us
  transfers between devices with their start and end apart: 6 -> 0, of which waited for: 4 -> 0; matrix products, arithmetic and copies ran while one was open for 13% -> 0% of each run, Pallas kernels for 0% -> 0%
where the time goes in v1:
time: 59.8 us; the launch traced here: 59.3 us
  Pallas kernels  46.8 us (78%)
  local copies, waits for them, and re-layouts  12.5 us (21%)
    pallas_call x1, Pallas kernels, body(): pl.pallas_call(kernel, out_shape=jax.ShapeDtypeStruct((REQ, OUT), BF16),...  46.8 us
    unnamed x29, local copies, waits for them, and re-layouts  12.5 us

profile of v1, /device:TPU:1, one launch (start us, length us, event | category | flops | bytes accessed | tf_op | source)
XLA Modules:
  0.0 59.3 jit_solution(6274831209134946946)
XLA Ops:
  0.0 0.0 copy-start
  0.0 1.2 %copy-done = bf16[32,128,128]{2,1,0:T(8,128)(2,1)S(1)} copy-done((bf16[32,128,128]{2,1,0:T(8,128)(2,1)S(1)}, bf16[32,128,128]{2,1,0:T(8,128)(2,1)}, u32[]{:S(2)}) %copy-start) | copy-done | bytes 1048600
  1.2 0.0 copy-start.1
  1.2 1.2 %copy-done.1 = bf16[32,128,128]{2,1,0:T(8,128)(2,1)S(1)} copy-done((bf16[32,128,128]{2,1,0:T(8,128)(2,1)S(1)}, bf16[32,128,128]{2,1,0:T(8,128)(2,1)}, u32[]{:S(2)}) %copy-start.1) | copy-done | bytes 1048600
  2.5 0.0 copy-start.2
  2.5 1.2 %copy-done.2 = bf16[8,64,1024]{2,1,0:T(8,128)(2,1)S(1)} copy-done((bf16[8,64,1024]{2,1,0:T(8,128)(2,1)S(1)}, bf16[8,64,1024]{2,1,0:T(8,128)(2,1)}, u32[]{:S(2)}) %copy-start.2) | copy-done | bytes 1048600
  3.7 0.0 copy-start.3
  3.7 1.0 %copy-done.3 = bf16[8,64,512]{2,1,0:T(8,128)(2,1)S(1)} copy-done((bf16[8,64,512]{2,1,0:T(8,128)(2,1)S(1)}, bf16[8,64,512]{2,1,0:T(8,128)(2,1)}, u32[]{:S(2)}) %copy-start.3) | copy-done | bytes 524312
  4.7 0.0 copy-start.4
  4.7 0.9 %copy-done.4 = bf16[1,64,1024]{2,1,0:T(8,128)(2,1)S(1)} copy-done((bf16[1,64,1024]{2,1,0:T(8,128)(2,1)S(1)}, bf16[1,64,1024]{2,1,0:T(8,128)(2,1)}, u32[]{:S(2)}) %copy-start.4) | copy-done | bytes 131096
  5.6 0.0 copy-start.5
  5.6 0.8 %copy-done.5 = bf16[1,64,512]{2,1,0:T(8,128)(2,1)S(1)} copy-done((bf16[1,64,512]{2,1,0:T(8,128)(2,1)S(1)}, bf16[1,64,512]{2,1,0:T(8,128)(2,1)}, u32[]{:S(2)}) %copy-start.5) | copy-done | bytes 65560
  6.5 0.0 copy-start.6
  6.5 0.8 %copy-done.6 = bf16[32,512]{1,0:T(8,128)(2,1)S(1)} copy-done((bf16[32,512]{1,0:T(8,128)(2,1)S(1)}, bf16[32,512]{1,0:T(8,128)(2,1)}, u32[]{:S(2)}) %copy-start.6) | copy-done | bytes 32792
  7.2 0.0 copy-start.7
  7.2 0.7 %copy-done.7 = bf16[32,128]{1,0:T(8,128)(2,1)S(1)} copy-done((bf16[32,128]{1,0:T(8,128)(2,1)S(1)}, bf16[32,128]{1,0:T(8,128)(2,1)}, u32[]{:S(2)}) %copy-start.7) | copy-done | bytes 8216
  7.9 0.0 copy-start.8
  7.9 0.7 %copy-done.8 = bf16[32,128]{1,0:T(8,128)(2,1)S(1)} copy-done((bf16[32,128]{1,0:T(8,128)(2,1)S(1)}, bf16[32,128]{1,0:T(8,128)(2,1)}, u32[]{:S(2)}) %copy-start.8) | copy-done | bytes 8216
  8.6 0.0 copy-start.9
  8.6 0.7 %copy-done.9 = s32[32]{0:T(128)S(1)} copy-done((s32[32]{0:T(128)S(1)}, s32[32]{0:T(128)}, u32[]{:S(2)}) %copy-start.9) | copy-done | bytes 152
  9.3 0.0 copy-start.10
  9.3 0.7 %copy-done.10 = s32[32]{0:T(128)S(1)} copy-done((s32[32]{0:T(128)S(1)}, s32[32]{0:T(128)}, u32[]{:S(2)}) %copy-start.10) | copy-done | bytes 152
  9.9 0.0 copy-start.11
  9.9 0.7 %copy-done.11 = s32[1,8]{1,0:T(1,128)S(1)} copy-done((s32[1,8]{1,0:T(1,128)S(1)}, s32[1,8]{1,0:T(1,128)}, u32[]{:S(2)}) %copy-start.11) | copy-done | bytes 56
  10.6 0.0 copy-start.12
  10.6 0.7 %copy-done.12 = s32[1,8]{1,0:T(1,128)S(1)} copy-done((s32[1,8]{1,0:T(1,128)S(1)}, s32[1,8]{1,0:T(1,128)}, u32[]{:S(2)}) %copy-start.12) | copy-done | bytes 56
  11.2 0.0 copy-start.13
  11.2 0.7 %copy-done.13 = s32[1,8]{1,0:T(1,128)S(1)} copy-done((s32[1,8]{1,0:T(1,128)S(1)}, s32[1,8]{1,0:T(1,128)}, u32[]{:S(2)}) %copy-start.13) | copy-done | bytes 56
  11.9 46.8 %shard_map.145 = bf16[32,1024]{1,0:T(8,128)(2,1)S(1)} custom-call(bf16[32,512]{1,0:T(8,128)(2,1)S(1)} %copy-done.6, bf16[32,128,128]{2,1,0:T(8,128)(2,1)S(1)} %copy-done, bf16[32,128,128]{2,1,0:T(8,128)(2,1)S(1)} %copy-done.1, bf16[32,128]{1,0:T(8,128)(2,1)S(1)} %copy-done.7, bf16[32,128]{1,0:T(8,128)(2,1)S(1)} %copy-done.8, s32[1,32]{1,0:T(1,128)S(1)} %bitcast.10, ...), custom_call_target="tpu_custom_call" | custom-call | tf_op jit(solution)/shard_map/pallas_call | solution.py:641
  58.7 0.6 %copy.17 = bf16[32,1024]{1,0:T(8,128)(2,1)} copy(bf16[32,1024]{1,0:T(8,128)(2,1)S(1)} %shard_map.145) | data formatting | bytes 131072
Async XLA Ops:
  0.0 1.2 %copy-start = (bf16[32,128,128]{2,1,0:T(8,128)(2,1)S(1)}, bf16[32,128,128]{2,1,0:T(8,128)(2,1)}, u32[]{:S(2)}) copy-start(bf16[32,128,128]{2,1,0:T(8,128)(2,1)} %k_hbm.1) | copy-start | bytes 3145732
  1.2 1.2 %copy-start.1 = (bf16[32,128,128]{2,1,0:T(8,128)(2,1)S(1)}, bf16[32,128,128]{2,1,0:T(8,128)(2,1)}, u32[]{:S(2)}) copy-start(bf16[32,128,128]{2,1,0:T(8,128)(2,1)} %v_hbm.1) | copy-start | bytes 3145732
  2.5 1.2 %copy-start.2 = (bf16[8,64,1024]{2,1,0:T(8,128)(2,1)S(1)}, bf16[8,64,1024]{2,1,0:T(8,128)(2,1)}, u32[]{:S(2)}) copy-start(bf16[8,64,1024]{2,1,0:T(8,128)(2,1)} %param.25) | copy-start | bytes 3145732
  3.7 1.0 %copy-start.3 = (bf16[8,64,512]{2,1,0:T(8,128)(2,1)S(1)}, bf16[8,64,512]{2,1,0:T(8,128)(2,1)}, u32[]{:S(2)}) copy-start(bf16[8,64,512]{2,1,0:T(8,128)(2,1)} %param.24) | copy-start | bytes 1572868
  4.7 0.9 %copy-start.4 = (bf16[1,64,1024]{2,1,0:T(8,128)(2,1)S(1)}, bf16[1,64,1024]{2,1,0:T(8,128)(2,1)}, u32[]{:S(2)}) copy-start(bf16[1,64,1024]{2,1,0:T(8,128)(2,1)} %param.27) | copy-start | bytes 393220
  5.6 0.8 %copy-start.5 = (bf16[1,64,512]{2,1,0:T(8,128)(2,1)S(1)}, bf16[1,64,512]{2,1,0:T(8,128)(2,1)}, u32[]{:S(2)}) copy-start(bf16[1,64,512]{2,1,0:T(8,128)(2,1)} %param.26) | copy-start | bytes 196612
  6.5 0.8 %copy-start.6 = (bf16[32,512]{1,0:T(8,128)(2,1)S(1)}, bf16[32,512]{1,0:T(8,128)(2,1)}, u32[]{:S(2)}) copy-start(bf16[32,512]{1,0:T(8,128)(2,1)} %q_ref.1) | copy-start | bytes 98308
  7.2 0.7 %copy-start.7 = (bf16[32,128]{1,0:T(8,128)(2,1)S(1)}, bf16[32,128]{1,0:T(8,128)(2,1)}, u32[]{:S(2)}) copy-start(bf16[32,128]{1,0:T(8,128)(2,1)} %nk_ref.1) | copy-start | bytes 24580
  7.9 0.7 %copy-start.8 = (bf16[32,128]{1,0:T(8,128)(2,1)S(1)}, bf16[32,128]{1,0:T(8,128)(2,1)}, u32[]{:S(2)}) copy-start(bf16[32,128]{1,0:T(8,128)(2,1)} %nv_ref.1) | copy-start | bytes 24580
  8.6 0.7 %copy-start.9 = (s32[32]{0:T(128)S(1)}, s32[32]{0:T(128)}, u32[]{:S(2)}) copy-start(s32[32]{0:T(128)} %param.20) | copy-start | bytes 388
  9.3 0.7 %copy-start.10 = (s32[32]{0:T(128)S(1)}, s32[32]{0:T(128)}, u32[]{:S(2)}) copy-start(s32[32]{0:T(128)} %param.29) | copy-start | bytes 388
  9.9 0.7 %copy-start.11 = (s32[1,8]{1,0:T(1,128)S(1)}, s32[1,8]{1,0:T(1,128)}, u32[]{:S(2)}) copy-start(s32[1,8]{1,0:T(1,128)} %send_s.1) | copy-start | bytes 100
  10.6 0.7 %copy-start.12 = (s32[1,8]{1,0:T(1,128)S(1)}, s32[1,8]{1,0:T(1,128)}, u32[]{:S(2)}) copy-start(s32[1,8]{1,0:T(1,128)} %recv_s.1) | copy-start | bytes 100
  11.2 0.7 %copy-start.13 = (s32[1,8]{1,0:T(1,128)S(1)}, s32[1,8]{1,0:T(1,128)}, u32[]{:S(2)}) copy-start(s32[1,8]{1,0:T(1,128)} %install_s.1) | copy-start | bytes 100

commit v2 on v1

--- a/solution.py
+++ b/solution.py
@@ -28,6 +28,7 @@
 OUT_PART = OUT // ROW
 SCALE = HD**-0.5
 DISTANCES = (1, 8, 12, 16)
+FAR_FIRST = (2, 0, 3, 1)
 
 
 def iota(shape, dim):
@@ -69,9 +70,23 @@
 
 
 def kernel(
-    q_ref,
+    q_hbm,
     k_hbm,
     v_hbm,
+    nk_hbm,
+    nv_hbm,
+    len_hbm,
+    slot_hbm,
+    send_hbm,
+    recv_hbm,
+    install_hbm,
+    w_hbm,
+    adown_hbm,
+    aup_hbm,
+    sdown_hbm,
+    sup_hbm,
+    out_ref,
+    q_ref,
     nk_ref,
     nv_ref,
     len_row,
@@ -80,12 +95,6 @@
     send_s,
     recv_s,
     install_s,
-    w_hbm,
-    adown_hbm,
-    aup_hbm,
-    sdown_hbm,
-    sup_hbm,
-    out_ref,
     kbuf,
     vbuf,
     wbuf,
@@ -98,7 +107,6 @@
     meta,
     res,
     mig,
-    loc,
     merged,
     obuf,
     fold,
@@ -114,6 +122,7 @@
     rs_own,
     rs_out,
     rs_in,
+    small_sem,
     load_sem,
     s1_local,
     s1_ssem,
@@ -148,24 +157,39 @@
     core = t % 2
     sib = (r, t + 1 - 2 * core)
 
+    other0 = y * 8 + (1 - zh) * 4
+    greeted = [((r + o) % REP, t) for o in (12, 20)]
+    greeted += [(other0 + (x + o) % 4, t) for o in (2, 1, 3, 0)]
+    greeted += [((r + o) % REP, t) for o in (1, 31, 16, 8, 24)]
+    greeted += [
+        (row0 + (x + xo) % 4, ((z + zo) % 4) * 2 + core)
+        for xo in (2, 1, 3, 0)
+        for zo in (2, 1, 3, 0)
+        if xo or zo
+    ]
+    greeted.append(sib)
     barrier = pltpu.get_barrier_semaphore()
-
-    def greet_rep(i, carry):
-        pl.semaphore_signal(
-            barrier, inc=1, device_id=((r + i) % REP, t), device_id_type=MESH
-        )
-        return carry
-
-    lax.fori_loop(1, REP, greet_rep, 0)
-
-    def greet_row(i, carry):
-        peer = (row0 + (x + i // 3) % 4, ((z + 1 + i % 3) % 4) * 2 + core)
+    for peer in greeted:
         pl.semaphore_signal(barrier, inc=1, device_id=peer, device_id_type=MESH)
-        return carry
-
-    lax.fori_loop(0, 12, greet_row, 0)
-    pl.semaphore_signal(barrier, inc=1, device_id=sib, device_id_type=MESH)
-
+
+    small = [
+        pltpu.make_async_copy(src, dst, small_sem.at[n])
+        for n, (src, dst) in enumerate(
+            (
+                (q_hbm, q_ref),
+                (nk_hbm, nk_ref),
+                (nv_hbm, nv_ref),
+                (recv_hbm, recv_s),
+                (install_hbm, install_s),
+                (slot_hbm, slot_row),
+                (len_hbm, len_row),
+                (len_hbm, len_s),
+                (send_hbm, send_s),
+            )
+        )
+    ]
+    for copy in small:
+        copy.start()
     k_load = pltpu.make_async_copy(k_hbm, kbuf, load_sem.at[0])
     v_load = pltpu.make_async_copy(v_hbm, vbuf, load_sem.at[1])
     ad_load = pltpu.make_async_copy(adown_hbm, adown, load_sem.at[2])
@@ -173,6 +197,8 @@
     au_load = pltpu.make_async_copy(aup_hbm, aup, load_sem.at[4])
     for copy in (k_load, v_load, ad_load, w_load, au_load):
         copy.start()
+    for copy in small:
+        copy.wait()
 
     queries = q_ref[...]
     q_heads = jnp.concatenate(
@@ -209,112 +235,8 @@
         target = jnp.where(slots == k, install_s[0, k], target)
     target = jnp.concatenate([target, jnp.full((1, 128 - REQ), -1, jnp.int32)], axis=1)
     sub8 = iota((8, 128), 0)
-    meta[x] = jnp.where(sub8 == 0, recv4, jnp.where(sub8 == 1, target, -1))
-
-    pl.semaphore_wait(barrier, 31 + 12 + 1)
-
-    sends = []
-
-    q_copies = []
-    for g, distance in enumerate(DISTANCES):
-        copy = remote(
-            qout.at[g],
-            qin.at[g],
-            q_ssem.at[g],
-            q_rsem.at[g],
-            ((r + REP - distance) % REP, t),
-        )
-        copy.start()
-        q_copies.append(copy)
-    sends += q_copies
-
-    my_dn = pl.ds(pl.multiple_of(r * RANK_PART, RANK_PART), RANK_PART)
-    my_up = pl.ds(pl.multiple_of(r * RANK, RANK), RANK)
-
-    def dn_part(c):
-        return sdown_hbm.at[pl.ds(pl.multiple_of(c * RANK_PART, RANK_PART), RANK_PART)]
-
-    def up_part(c):
-        return sup_hbm.at[:, pl.ds(pl.multiple_of(c * OUT_PART, OUT_PART), OUT_PART)]
-
-    own_dn = pltpu.make_async_copy(dn_part(x), sdn.at[my_dn], s1_local.at[0])
-    own_up = pltpu.make_async_copy(up_part(x), sup.at[my_up], s1_local.at[1])
-    own_dn.start()
-    own_up.start()
-    near_dn, near_up, far_dn, far_up = [], [], [], []
-    for o in range(1, 4):
-        c = (x + o) % 4
-        near_dn.append(
-            remote(dn_part(c), sdn.at[my_dn], s1_ssem.at[0, o], s1_rsem.at[0, o], (row0 + c, t))
-        )
-        near_up.append(
-            remote(up_part(c), sup.at[my_up], s1_ssem.at[1, o], s1_rsem.at[1, o], (row0 + c, t))
-        )
-    other0 = y * 8 + (1 - zh) * 4
-    for o in range(4):
-        c = (x + o) % 4
-        far_dn.append(
-            remote(dn_part(c), sdn.at[my_dn], s1_ssem.at[2, o], s1_rsem.at[2, o], (other0 + c, t))
-        )
-        far_up.append(
-            remote(up_part(c), sup.at[my_up], s1_ssem.at[3, o], s1_rsem.at[3, o], (other0 + c, t))
-        )
-    for copy in far_dn + near_dn + near_up + far_up:
-        copy.start()
-    sends += near_dn + near_up + far_dn + far_up
-
-    meta_copies = []
-    for o in range(1, 4):
-        copy = remote(
-            meta.at[x], meta.at[x], meta_ssem.at[o], meta_rsem.at[o], (row0 + (x + o) % 4, t)
-        )
-        copy.start()
-        meta_copies.append(copy)
-    sends += meta_copies
-
-    def stage2(half, tag):
-        first = y * 8 + half * 4
-        dn_rows = pl.ds(pl.multiple_of(first * RANK_PART, 4 * RANK_PART), 4 * RANK_PART)
-        up_rows = pl.ds(pl.multiple_of(first * RANK, 4 * RANK), 4 * RANK)
-        dn, up = [], []
-        for o in range(1, 4):
-            peer = ((r + 8 * o) % REP, t)
-            dn.append(
-                remote(
-                    sdn.at[dn_rows], sdn.at[dn_rows], s2_ssem.at[tag, o], s2_rsem.at[tag, o], peer
-                )
-            )
-            up.append(
-                remote(
-                    sup.at[up_rows],
-                    sup.at[up_rows],
-                    s2_ssem.at[2 + tag, o],
-                    s2_rsem.at[2 + tag, o],
-                    peer,
-                )
-            )
-        return dn, up
-
-    s2_near_dn, s2_near_up = stage2(zh, 0)
-    s2_far_dn, s2_far_up = stage2(1 - zh, 1)
-    sends += s2_near_dn + s2_near_up + s2_far_dn + s2_far_up
-
-    fc = iota((5 * 512, 128), 0)
-    fl = iota((5 * 512, 128), 1)
-    block = fc // 512
-    goal = jnp.where(block < 4, block * RANK_PART + fc % RANK_PART, 64 + fc % RANK)
-    fold[...] = (fl == goal).astype(BF16)
-    pc = iota((512, 512), 0)
-    pj = iota((512, 512), 1)
-    inner = pc % 128
-    hit = (
-        (inner < 64)
-        & (inner // RANK_PART == pj // 128)
-        & (pj % 64 == (pc // 128) * RANK_PART + pc % RANK_PART)
-    )
-    perm[...] = hit.astype(BF16)
-
-    own_dn.wait()
+    meta[x] = jnp.where(sub8 == 1, target, -1)
+
     k_load.wait()
     er = iota((256, 128), 0)
     ec = iota((256, 128), 1)
@@ -341,17 +263,165 @@
         preferred_element_type=F32,
     ).reshape(256, HD)
     obuf[...] = (summed + own_b * new_kv[:, HD:]) / total
-    for h in range(HEADS):
-        loc[x, :, h * HD : (h + 1) * HD] = obuf[pl.ds(h, REQ, stride=8), :].astype(BF16)
-
-    loc_copies = []
+    here = jnp.concatenate(
+        [obuf[pl.ds(h, REQ, stride=8), :] for h in range(HEADS)], axis=1
+    ).astype(BF16)
+
+    fc = iota((5 * 512, 128), 0)
+    fl = iota((5 * 512, 128), 1)
+    block = fc // 512
+    goal = jnp.where(block < 4, block * RANK_PART + fc % RANK_PART, 64 + fc % RANK)
+    fold[...] = (fl == goal).astype(BF16)
+    pc = iota((512, 512), 0)
+    pj = iota((512, 512), 1)
+    inner = pc % 128
+    hit = (
+        (inner < 64)
+        & (inner // RANK_PART == pj // 128)
+        & (pj % 64 == (pc // 128) * RANK_PART + pc % RANK_PART)
+    )
+    perm[...] = hit.astype(BF16)
+
+    pl.semaphore_wait(barrier, len(greeted))
+
+    sends = []
+
+    q_copies = []
+    for g in FAR_FIRST:
+        copy = remote(
+            qout.at[g],
+            qin.at[g],
+            q_ssem.at[g],
+            q_rsem.at[g],
+            ((r + REP - DISTANCES[g]) % REP, t),
+        )
+        copy.start()
+        q_copies.append(copy)
+    sends += q_copies
+
+    my_dn = pl.ds(pl.multiple_of(r * RANK_PART, RANK_PART), RANK_PART)
+    my_up = pl.ds(pl.multiple_of(r * RANK, RANK), RANK)
+
+    def dn_part(c):
+        return sdown_hbm.at[pl.ds(pl.multiple_of(c * RANK_PART, RANK_PART), RANK_PART)]
+
+    def up_part(c):
+        return sup_hbm.at[:, pl.ds(pl.multiple_of(c * OUT_PART, OUT_PART), OUT_PART)]
+
+    own_dn = pltpu.make_async_copy(dn_part(x), sdn.at[my_dn], s1_local.at[0])
+    own_up = pltpu.make_async_copy(up_part(x), sup.at[my_up], s1_local.at[1])
+    own_dn.start()
+    own_up.start()
+    near_dn, near_up, far_dn, far_up = [], [], [], []
+    for o in range(1, 4):
+        c = (x + o) % 4
+        near_dn.append(
+            remote(dn_part(c), sdn.at[my_dn], s1_ssem.at[0, o], s1_rsem.at[0, o], (row0 + c, t))
+        )
+        near_up.append(
+            remote(up_part(c), sup.at[my_up], s1_ssem.at[1, o], s1_rsem.at[1, o], (row0 + c, t))
+        )
+    for o in range(4):
+        c = (x + o) % 4
+        far_dn.append(
+            remote(dn_part(c), sdn.at[my_dn], s1_ssem.at[2, o], s1_rsem.at[2, o], (other0 + c, t))
+        )
+        far_up.append(
+            remote(up_part(c), sup.at[my_up], s1_ssem.at[3, o], s1_rsem.at[3, o], (other0 + c, t))
+        )
+    for copy in far_dn + near_dn + near_up + far_up:
+        copy.start()
+    sends += near_dn + near_up + far_dn + far_up
+
+    meta_copies = []
     for o in range(1, 4):
         copy = remote(
-            loc.at[x], loc.at[x], loc_ssem.at[o], loc_rsem.at[o], (row0 + (x + o) % 4, t)
-        )
-        copy.start()
-        loc_copies.append(copy)
-    sends += loc_copies
+            meta.at[x], meta.at[x], meta_ssem.at[o], meta_rsem.at[o], (row0 + (x + o) % 4, t)
+        )
+        copy.start()
+        meta_copies.append(copy)
+    sends += meta_copies
+
+    def stage2(half, tag):
+        first = y * 8 + half * 4
+        dn_rows = pl.ds(pl.multiple_of(first * RANK_PART, 4 * RANK_PART), 4 * RANK_PART)
+        up_rows = pl.ds(pl.multiple_of(first * RANK, 4 * RANK), 4 * RANK)
+        dn, up = [], []
+        for o in range(1, 4):
+            peer = ((r + 8 * o) % REP, t)
+            dn.append(
+                remote(
+                    sdn.at[dn_rows], sdn.at[dn_rows], s2_ssem.at[tag, o], s2_rsem.at[tag, o], peer
+                )
+            )
+            up.append(
+                remote(
+                    sup.at[up_rows],
+                    sup.at[up_rows],
+                    s2_ssem.at[2 + tag, o],
+                    s2_rsem.at[2 + tag, o],
+                    peer,
+                )
+            )
+        return dn, up
+
+    s2_near_dn, s2_near_up = stage2(zh, 0)
+    s2_far_dn, s2_far_up = stage2(1 - zh, 1)
+    sends += s2_near_dn + s2_near_up + s2_far_dn + s2_far_up
+
+    order = (2, 1, 3, 0)
+
+    class Wave:
+        def __init__(self, rows, own, sib_out, sib_in, out, arriving, sems):
+            self.rows, self.own, self.out, self.arriving = rows, own, out, arriving
+            self.sib_out, self.sib_in, self.sems = sib_out, sib_in, sems
+            self.sib_copies, self.copies = [], []
+
+        def project(self, zq, cq):
+            first = pl.multiple_of((zq * 2 + cq) * OUT, OUT)
+            return dot_nt(self.rows, wbuf[pl.ds(first, OUT), :])
+
+        def opposite(self, n):
+            self.sib_out[n] = self.project((z + order[n]) % 4, 1 - core).astype(BF16)
+            copy = remote(
+                self.sib_out.at[n], self.sib_in.at[n], self.sems[0].at[n], self.sems[1].at[n], sib
+            )
+            copy.start()
+            self.sib_copies.append(copy)
+
+        def same(self, n):
+            self.own[n] = self.project((z + order[n]) % 4, core)
+
+        def pass_on(self, n):
+            zq = (z + order[n]) % 4
+            self.sib_copies[n].wait_recv()
+            both = self.own[n] + self.sib_in[n].astype(F32)
+            if order[n] == 0:
+                self.own[n] = both
+                return
+            self.out[n] = both.astype(BF16)
+            copy = remote(
+                self.out.at[n],
+                self.arriving.at[n],
+                self.sems[2].at[n],
+                self.sems[3].at[n],
+                (r, zq * 2 + core),
+            )
+            copy.start()
+            self.copies.append(copy)
+
+        def total(self):
+            acc = self.own[3]
+            for n, copy in enumerate(self.copies):
+                copy.wait_recv()
+                acc = acc + self.arriving[n].astype(F32)
+            return acc
+
+    own_dn.wait()
+    for copy in near_dn:
+        copy.wait_recv()
+    for copy in s2_near_dn:
+        copy.start()
 
     for copy in q_copies:
         copy.wait_recv()
@@ -393,36 +463,19 @@
     for g in range(SPAN):
         res[g] = m_out[g * 8 : (g + 1) * 8]
 
-    mig_sends = []
-    for g, distance in enumerate(DISTANCES):
-        home = (r + distance) % REP
-        home_x = home % 4
-        for c in range(ROW):
-            device = home - home_x + c
-            dst = mig.at[home_x, pl.ds(8 * g, 8)]
-            copy = remote(
-                res.at[g], dst, mig_ssem.at[g, c], mig_rsem.at[home_x, g], (device, t)
-            )
-            if g == 0:
-                here = pltpu.make_async_copy(res.at[g], dst, mig_rsem.at[home_x, g])
-
-                @pl.when(device == r)
-                def _():
-                    here.start()
-
-                @pl.when(device != r)
-                def _():
-                    copy.start()
-
-                mig_sends.append((copy, device))
-            else:
-                copy.start()
-                sends.append(copy)
-
-    for copy in near_dn:
-        copy.wait_recv()
-    for copy in s2_near_dn:
-        copy.start()
+    mig_copies = []
+    for g in FAR_FIRST:
+        copy = remote(
+            res.at[g],
+            mig.at[pl.ds(8 * g, 8)],
+            mig_ssem.at[g],
+            mig_rsem.at[g],
+            ((r + DISTANCES[g]) % REP, t),
+        )
+        copy.start()
+        mig_copies.append(copy)
+    sends += mig_copies
+
     for copy in far_dn:
         copy.wait_recv()
     for copy in s2_far_dn:
@@ -433,85 +486,57 @@
     for copy in s2_near_up:
         copy.start()
 
-    for copy in meta_copies:
-        copy.wait_recv()
-    for copy in loc_copies:
-        copy.wait_recv()
-    for h in range(ROW):
-        for g in range(SPAN):
-            remote(res.at[0], mig.at[h, pl.ds(8 * g, 8)], mig_ssem.at[g, 0], mig_rsem.at[h, g], sib).wait_recv()
+    for copy in mig_copies:
+        copy.wait_recv()
     mh = iota((128, 32), 0)
-    ml = iota((128, 32), 1)
-    tcols = []
-    for h in range(ROW):
-        tile = meta[h]
-        tcols.append(to_column(tile[1:2], REQ))
-        recv_row = tile[0:1, 0:32]
-        put = ((mh % REQ == recv_row) & (mh // REQ == ml % 4)).astype(BF16)
-        rows = dot(put, mig[h].astype(BF16)).astype(BF16)
-        taken = jnp.max(
-            jnp.where(iota((REQ, 32), 0) == recv_row, 1.0, 0.0), axis=1, keepdims=True
-        )
-        here = loc[h]
-        for k in range(HEADS):
-            span = slice(k * HD, (k + 1) * HD)
-            merged[h * REQ : (h + 1) * REQ, span] = jnp.where(
-                taken > 0.5, rows[k * REQ : (k + 1) * REQ], here[:, span]
-            )
-
-    mine = merged[pl.ds(pl.multiple_of(x * REQ, REQ), REQ), :]
-
+    put = ((mh % REQ == recv4[:, 0:32]) & (mh // REQ == iota((128, 32), 1) % 4)).astype(BF16)
+    rows = dot(put, mig[...].astype(BF16)).astype(BF16)
+    taken = (
+        jnp.max(
+            jnp.where(iota((REQ, 32), 0) == recv4[:, 0:32], 1.0, 0.0), axis=1, keepdims=True
+        )
+        > 0.5
+    )
+    mine = jnp.where(
+        taken,
+        jnp.concatenate([rows[k * REQ : (k + 1) * REQ] for k in range(HEADS)], axis=1),
+        here,
+    )
+    my_rows = pl.ds(pl.multiple_of(x * REQ, REQ), REQ)
+    merged[my_rows, :] = mine
+    row_copies = []
+    for o in (2, 1, 3):
+        copy = remote(
+            merged.at[my_rows],
+            merged.at[my_rows],
+            loc_ssem.at[o],
+            loc_rsem.at[o],
+            (row0 + (x + o) % 4, t),
+        )
+        copy.start()
+        row_copies.append(copy)
+    sends += row_copies
+
+    proj = Wave(
+        mine, rs_own, sib_out, sib_in, rs_out, rs_in, (sib_ssem, sib_rsem, rs_ssem, rs_rsem)
+    )
     w_load.wait()
-
-    def project(zq, cq):
-        first = pl.multiple_of((zq * 2 + cq) * OUT, OUT)
-        return dot_nt(mine, wbuf[pl.ds(first, OUT), :])
-
-    sib_copies = []
-    rs_copies = []
-    order = (2, 1, 3, 0)
-
-    def opposite(n):
-        zq = (z + order[n]) % 4
-        sib_out[n] = project(zq, 1 - core).astype(BF16)
-        copy = remote(sib_out.at[n], sib_in.at[n], sib_ssem.at[n], sib_rsem.at[n], sib)
-        copy.start()
-        sib_copies.append(copy)
-
-    def same(n):
-        rs_own[n] = project((z + order[n]) % 4, core)
-
-    def pass_on(n):
-        zq = (z + order[n]) % 4
-        sib_copies[n].wait_recv()
-        both = rs_own[n] + sib_in[n].astype(F32)
-        if order[n] == 0:
-            rs_own[n] = both
-            return
-        rs_out[n] = both.astype(BF16)
-        copy = remote(
-            rs_out.at[n], rs_in.at[n], rs_ssem.at[n], rs_rsem.at[n], (r, zq * 2 + core)
-        )
-        copy.start()
-        rs_copies.append(copy)
-
-    opposite(0)
-    same(0)
-    opposite(1)
-    pass_on(0)
-    same(1)
+    proj.opposite(0)
+    proj.same(0)
+    proj.opposite(1)
+    proj.pass_on(0)
 
     ad_load.wait()
     slot_col = to_column(
         jnp.concatenate([slots, jnp.full((1, 128 - REQ), -1, jnp.int32)], axis=1), REQ
     )
-    target_col = to_column(meta[x][1:2], REQ)
-    resident = target_col < 0
+    resident = to_column(target, REQ) < 0
     c512 = iota((REQ, 512), 1)
     part = dot_nt(mine, adown[...])
     pieces = [jnp.where((c512 // RANK == slot_col) & resident, part, 0.0)]
-    for copy in s2_near_dn + s2_far_dn:
-        copy.wait_recv()
+    for copy in meta_copies + row_copies + s2_near_dn + s2_far_dn:
+        copy.wait_recv()
+    tcols = [to_column(meta[h][1:2], REQ) for h in range(ROW)]
     part = dot_nt(merged[...], sdn[...])
     sections = [
         jnp.where(c512 // RANK_PART == tcols[h], part[h * REQ : (h + 1) * REQ], 0.0)
@@ -525,8 +550,9 @@
         copy.wait_recv()
     for copy in s2_far_up:
         copy.start()
-    opposite(2)
-    pass_on(1)
+    proj.same(1)
+    proj.opposite(2)
+    proj.pass_on(1)
     msg_copy.wait_recv()
     bc[x, z] = (msg[0].astype(F32) + msg_sib[...].astype(F32)).astype(BF16)
     bc_copies = []
@@ -544,11 +570,11 @@
             copy.start()
             bc_copies.append(copy)
     sends += bc_copies
-    same(2)
-    opposite(3)
-    pass_on(2)
-    same(3)
-    pass_on(3)
+    proj.same(2)
+    proj.opposite(3)
+    proj.pass_on(2)
+    proj.same(3)
+    proj.pass_on(3)
 
     for copy in bc_copies:
         copy.wait_recv()
@@ -594,12 +620,7 @@
         ],
         axis=1,
     ).astype(BF16)
-    acc = dot(spread, aup[...]) + rs_own[3]
-
-    for copy in rs_copies:
-        copy.wait_recv()
-    for n in range(3):
-        acc = acc + rs_in[n].astype(F32)
+    acc = dot(spread, aup[...]) + proj.total()
     for copy in dlt_copies:
         copy.wait_recv()
     out_ref[...] = (
@@ -607,13 +628,8 @@
     ).astype(BF16)
 
     msg_copy.wait_send()
-    for copy in sib_copies + rs_copies + sends:
+    for copy in proj.sib_copies + proj.copies + sends:
         copy.wait_send()
-    for copy, device in mig_sends:
-
-        @pl.when(device != r)
-        def _():
-            copy.wait_send()
 
 
 def body(
@@ -634,17 +650,25 @@
     adapter_slot,
 ):
     vmem = pl.BlockSpec(memory_space=pltpu.VMEM)
-    smem = pl.BlockSpec(memory_space=pltpu.SMEM)
-    hbm = pl.BlockSpec(memory_space=pl.ANY)
+    hbm = pl.BlockSpec(memory_space=pltpu.HBM)
+    smem = functools.partial(pltpu.SMEM, dtype=jnp.int32)
     dma = pltpu.SemaphoreType.DMA
     lengths = kv_len.reshape(1, REQ)
     return pl.pallas_call(
         kernel,
         out_shape=jax.ShapeDtypeStruct((REQ, OUT), BF16),
-        in_specs=[vmem, hbm, hbm, vmem, vmem, vmem, vmem, smem, smem, smem, smem]
-        + [hbm] * 5,
+        in_specs=[hbm] * 15,
         out_specs=vmem,
         scratch_shapes=[
+            pltpu.VMEM((REQ, QW), BF16),
+            pltpu.VMEM((REQ, HD), BF16),
+            pltpu.VMEM((REQ, HD), BF16),
+            pltpu.VMEM((1, REQ), jnp.int32),
+            pltpu.VMEM((1, REQ), jnp.int32),
+            smem((1, REQ)),
+            smem((1, SPAN * CAP)),
+            smem((1, SPAN * CAP)),
+            smem((1, SLOTS)),
             pltpu.VMEM((REQ, LMAX, HD), BF16),
             pltpu.VMEM((REQ, LMAX, HD), BF16),
             pltpu.VMEM((TP * OUT, QW), BF16),
@@ -656,8 +680,7 @@
             pltpu.VMEM((SPAN, 16, HD), BF16),
             pltpu.VMEM((ROW, 8, 128), jnp.int32),
             pltpu.VMEM((SPAN, 8, HD), F32),
-            pltpu.VMEM((ROW, 32, HD), F32),
-            pltpu.VMEM((ROW, REQ, QW), BF16),
+            pltpu.VMEM((32, HD), F32),
             pltpu.VMEM((ROW * REQ, QW), BF16),
             pltpu.VMEM((256, HD), F32),
             pltpu.VMEM((5 * 512, 128), BF16),
@@ -673,6 +696,7 @@
             pltpu.VMEM((4, REQ, OUT), F32),
             pltpu.VMEM((3, REQ, OUT), BF16),
             pltpu.VMEM((3, REQ, OUT), BF16),
+            dma((9,)),
             dma((5,)),
             dma((2,)),
             dma((4, 4)),
@@ -683,8 +707,8 @@
             dma((4,)),
             dma((4,)),
             dma((4,)),
-            dma((4, 4)),
-            dma((4, 4)),
+            dma((4,)),
+            dma((4,)),
             dma((4,)),
             dma((4,)),
             dma((2,)),
@@ -698,7 +722,7 @@
             dma((4,)),
         ],
         compiler_params=pltpu.CompilerParams(
-            collective_id=0, has_side_effects=True, vmem_limit_bytes=48 << 20
+            collective_id=0, has_side_effects=True, vmem_limit_bytes=60 << 20
         ),
     )(
         queries,
@@ -708,7 +732,6 @@
         new_values,
         lengths,
         adapter_slot.reshape(1, REQ),
-        lengths,
         send_rows,
         recv_rows,
         install,

time: 59.8 us -> 47.5 us (0.79)
  local copies, waits for them, and re-layouts: 12.5 us -> 1.47 us
  Pallas kernels: 46.8 us -> 45.9 us
    unnamed x29 -> x1, local copies, waits for them, and re-layouts: 12.5 us -> 1.47 us
    pallas_call x1, Pallas kernels: 46.8 us -> 45.9 us  [body(): pl.pallas_call(kernel, out_shape=jax.ShapeDtypeStruct((REQ, OUT), BF16),...]
where the time goes in v2:
time: 47.5 us; the launch traced here: 47.3 us
  Pallas kernels  45.9 us (97%)
  local copies, waits for them, and re-layouts  1.47 us (3%)
    pallas_call x1, Pallas kernels, body(): pl.pallas_call(kernel, out_shape=jax.ShapeDtypeStruct((REQ, OUT), BF16),...  45.9 us
    unnamed x1, local copies, waits for them, and re-layouts  1.47 us

profile of v2, /device:TPU:1, one launch (start us, length us, event | category | flops | bytes accessed | tf_op | source)
XLA Modules:
  0.0 47.3 jit_solution(8981515058407291656)
XLA Ops:
  0.0 45.9 %shard_map.145 = bf16[32,1024]{1,0:T(8,128)(2,1)} custom-call(bf16[32,512]{1,0:T(8,128)(2,1)} %q_hbm.1, bf16[32,128,128]{2,1,0:T(8,128)(2,1)} %k_hbm.1, bf16[32,128,128]{2,1,0:T(8,128)(2,1)} %v_hbm.1, bf16[32,128]{1,0:T(8,128)(2,1)} %nk_hbm.1, bf16[32,128]{1,0:T(8,128)(2,1)} %nv_hbm.1, s32[1,32]{1,0:T(1,128)} %bitcast.10, s32[1,32]{1,0:T(1,128)} %bitcast.11, ...), custom_call_target="tpu_custom_call" | custom-call | tf_op jit(solution)/shard_map/pallas_call | solution.py:657
  45.9 1.5 %copy.17 = bf16[32,1024]{1,0:T(8,128)(2,1)} copy(bf16[32,1024]{1,0:T(8,128)(2,1)} %shard_map.145) | data formatting | bytes 131072

commit v3 on v2

--- a/solution.py
+++ b/solution.py
@@ -52,6 +52,11 @@
         device_id=device,
         device_id_type=MESH,
     )
+
+
+def hops(offset):
+    dy, dx = offset // 8, offset % 4
+    return min(dy, 4 - dy) + min(dx, 4 - dx) + 4 * ((offset // 4) % 2)
 
 
 def softmax_parts(scores, own, live):
@@ -122,6 +127,11 @@
     rs_own,
     rs_out,
     rs_in,
+    sib2_out,
+    sib2_in,
+    rs2_own,
+    rs2_out,
+    rs2_in,
     small_sem,
     load_sem,
     s1_local,
@@ -146,6 +156,10 @@
     sib_rsem,
     rs_ssem,
     rs_rsem,
+    sib2_ssem,
+    sib2_rsem,
+    rs2_ssem,
+    rs2_rsem,
 ):
     r = lax.axis_index("rep")
     t = lax.axis_index("tp")
@@ -158,14 +172,11 @@
     sib = (r, t + 1 - 2 * core)
 
     other0 = y * 8 + (1 - zh) * 4
-    greeted = [((r + o) % REP, t) for o in (12, 20)]
-    greeted += [(other0 + (x + o) % 4, t) for o in (2, 1, 3, 0)]
-    greeted += [((r + o) % REP, t) for o in (1, 31, 16, 8, 24)]
+    greeted = [((r + o) % REP, t) for o in sorted(range(1, REP), key=hops, reverse=True)]
     greeted += [
         (row0 + (x + xo) % 4, ((z + zo) % 4) * 2 + core)
         for xo in (2, 1, 3, 0)
-        for zo in (2, 1, 3, 0)
-        if xo or zo
+        for zo in (2, 1, 3)
     ]
     greeted.append(sib)
     barrier = pltpu.get_barrier_semaphore()
@@ -235,52 +246,7 @@
         target = jnp.where(slots == k, install_s[0, k], target)
     target = jnp.concatenate([target, jnp.full((1, 128 - REQ), -1, jnp.int32)], axis=1)
     sub8 = iota((8, 128), 0)
-    meta[x] = jnp.where(sub8 == 1, target, -1)
-
-    k_load.wait()
-    er = iota((256, 128), 0)
-    ec = iota((256, 128), 1)
-    spread_q = ((er % 8 == ec // REQ) & (er // 8 == ec % REQ)).astype(BF16)
-    q_local = dot(spread_q, q_heads)
-    spread_r = iota((256, REQ), 0) // 8 == iota((256, REQ), 1)
-    new_kv = dot(spread_r.astype(BF16), jnp.concatenate([new_keys, new_values], axis=1))
-    lengths = jnp.sum(
-        jnp.where(spread_r, len_row[...], 0).astype(F32), axis=1, keepdims=True
-    ).astype(jnp.int32)
-    scores = lax.dot_general(
-        q_local.reshape(REQ, 8, HD).astype(BF16),
-        kbuf[...],
-        (((2,), (2,)), ((0,), (0,))),
-        preferred_element_type=F32,
-    ).reshape(256, LMAX)
-    own = jnp.sum(q_local * new_kv[:, :HD], axis=1, keepdims=True)
-    weights, own_b, total = softmax_parts(scores, own, ec < lengths)
-    v_load.wait()
-    summed = lax.dot_general(
-        weights.reshape(REQ, 8, LMAX),
-        vbuf[...],
-        (((2,), (1,)), ((0,), (0,))),
-        preferred_element_type=F32,
-    ).reshape(256, HD)
-    obuf[...] = (summed + own_b * new_kv[:, HD:]) / total
-    here = jnp.concatenate(
-        [obuf[pl.ds(h, REQ, stride=8), :] for h in range(HEADS)], axis=1
-    ).astype(BF16)
-
-    fc = iota((5 * 512, 128), 0)
-    fl = iota((5 * 512, 128), 1)
-    block = fc // 512
-    goal = jnp.where(block < 4, block * RANK_PART + fc % RANK_PART, 64 + fc % RANK)
-    fold[...] = (fl == goal).astype(BF16)
-    pc = iota((512, 512), 0)
-    pj = iota((512, 512), 1)
-    inner = pc % 128
-    hit = (
-        (inner < 64)
-        & (inner // RANK_PART == pj // 128)
-        & (pj % 64 == (pc // 128) * RANK_PART + pc % RANK_PART)
-    )
-    perm[...] = hit.astype(BF16)
+    meta[x] = jnp.where(sub8 == 0, recv4, jnp.where(sub8 == 1, target, -1))
 
     pl.semaphore_wait(barrier, len(greeted))
 
@@ -329,7 +295,7 @@
         far_up.append(
             remote(up_part(c), sup.at[my_up], s1_ssem.at[3, o], s1_rsem.at[3, o], (other0 + c, t))
         )
-    for copy in far_dn + near_dn + near_up + far_up:
+    for copy in far_dn + near_dn + near_up:
         copy.start()
     sends += near_dn + near_up + far_dn + far_up
 
@@ -382,7 +348,7 @@
             return dot_nt(self.rows, wbuf[pl.ds(first, OUT), :])
 
         def opposite(self, n):
-            self.sib_out[n] = self.project((z + order[n]) % 4, 1 - core).astype(BF16)
+            self.sib_out[n] = self.fit(self.project((z + order[n]) % 4, 1 - core)).astype(BF16)
             copy = remote(
                 self.sib_out.at[n], self.sib_in.at[n], self.sems[0].at[n], self.sems[1].at[n], sib
             )
@@ -390,7 +356,7 @@
             self.sib_copies.append(copy)
 
         def same(self, n):
-            self.own[n] = self.project((z + order[n]) % 4, core)
+            self.own[n] = self.fit(self.project((z + order[n]) % 4, core))
 
         def pass_on(self, n):
             zq = (z + order[n]) % 4
@@ -417,12 +383,18 @@
                 acc = acc + self.arriving[n].astype(F32)
             return acc
 
+        def fit(self, block):
+            if block.shape[0] == REQ:
+                return block
+            return jnp.concatenate([block[:8, : OUT // 2], block[:8, OUT // 2 :]], axis=0)
+
     own_dn.wait()
     for copy in near_dn:
         copy.wait_recv()
     for copy in s2_near_dn:
         copy.start()
 
+    k_load.wait()
     for copy in q_copies:
         copy.wait_recv()
     head8 = iota((8, HD), 0) // HEADS == 0
@@ -449,6 +421,7 @@
         jnp.concatenate(moved_own, axis=0),
         iota((32, 128), 1) < moved_len,
     )
+    v_load.wait()
     m_summed = []
     m_wf = m_weights.astype(F32)
     for g in range(SPAN):
@@ -463,47 +436,79 @@
     for g in range(SPAN):
         res[g] = m_out[g * 8 : (g + 1) * 8]
 
-    mig_copies = []
+    own_results = []
     for g in FAR_FIRST:
-        copy = remote(
-            res.at[g],
-            mig.at[pl.ds(8 * g, 8)],
-            mig_ssem.at[g],
-            mig_rsem.at[g],
-            ((r + DISTANCES[g]) % REP, t),
-        )
-        copy.start()
-        mig_copies.append(copy)
-    sends += mig_copies
-
-    for copy in far_dn:
-        copy.wait_recv()
-    for copy in s2_far_dn:
-        copy.start()
-    own_up.wait()
-    for copy in near_up:
-        copy.wait_recv()
-    for copy in s2_near_up:
-        copy.start()
-
-    for copy in mig_copies:
-        copy.wait_recv()
-    mh = iota((128, 32), 0)
-    put = ((mh % REQ == recv4[:, 0:32]) & (mh // REQ == iota((128, 32), 1) % 4)).astype(BF16)
-    rows = dot(put, mig[...].astype(BF16)).astype(BF16)
-    taken = (
-        jnp.max(
-            jnp.where(iota((REQ, 32), 0) == recv4[:, 0:32], 1.0, 0.0), axis=1, keepdims=True
-        )
-        > 0.5
-    )
-    mine = jnp.where(
-        taken,
-        jnp.concatenate([rows[k * REQ : (k + 1) * REQ] for k in range(HEADS)], axis=1),
-        here,
-    )
+        home = (r + DISTANCES[g]) % REP
+        home_x = home % 4
+        dst = mig.at[home_x, pl.ds(8 * g, 8)]
+        for o in (2, 1, 3, 0):
+            device = home - home_x + (home_x + o) % 4
+            copy = remote(
+                res.at[g], dst, mig_ssem.at[g, o], mig_rsem.at[home_x, g], (device, t)
+            )
+            if g == 0 and o:
+                stays = pltpu.make_async_copy(res.at[g], dst, mig_rsem.at[home_x, g])
+
+                @pl.when(device == r)
+                def _():
+                    stays.start()
+
+                @pl.when(device != r)
+                def _():
+                    copy.start()
+
+                own_results.append((copy, device))
+            else:
+                copy.start()
+                sends.append(copy)
+    for copy in far_up:
+        copy.start()
+
+    er = iota((256, 128), 0)
+    ec = iota((256, 128), 1)
+    spread_q = ((er % 8 == ec // REQ) & (er // 8 == ec % REQ)).astype(BF16)
+    q_local = dot(spread_q, q_heads)
+    spread_r = iota((256, REQ), 0) // 8 == iota((256, REQ), 1)
+    new_kv = dot(spread_r.astype(BF16), jnp.concatenate([new_keys, new_values], axis=1))
+    lengths = jnp.sum(
+        jnp.where(spread_r, len_row[...], 0).astype(F32), axis=1, keepdims=True
+    ).astype(jnp.int32)
+    scores = lax.dot_general(
+        q_local.reshape(REQ, 8, HD).astype(BF16),
+        kbuf[...],
+        (((2,), (2,)), ((0,), (0,))),
+        preferred_element_type=F32,
+    ).reshape(256, LMAX)
+    own = jnp.sum(q_local * new_kv[:, :HD], axis=1, keepdims=True)
+    weights, own_b, total = softmax_parts(scores, own, ec < lengths)
+    summed = lax.dot_general(
+        weights.reshape(REQ, 8, LMAX),
+        vbuf[...],
+        (((2,), (1,)), ((0,), (0,))),
+        preferred_element_type=F32,
+    ).reshape(256, HD)
+    obuf[...] = (summed + own_b * new_kv[:, HD:]) / total
+    here = jnp.concatenate(
+        [obuf[pl.ds(h, REQ, stride=8), :] for h in range(HEADS)], axis=1
+    ).astype(BF16)
+
+    fc = iota((5 * 512, 128), 0)
+    fl = iota((5 * 512, 128), 1)
+    block = fc // 512
+    goal = jnp.where(block < 4, block * RANK_PART + fc % RANK_PART, 64 + fc % RANK)
+    fold[...] = (fl == goal).astype(BF16)
+    pc = iota((512, 512), 0)
+    pj = iota((512, 512), 1)
+    inner = pc % 128
+    hit = (
+        (inner < 64)
+        & (inner // RANK_PART == pj // 128)
+        & (pj % 64 == (pc // 128) * RANK_PART + pc % RANK_PART)
+    )
+    perm[...] = hit.astype(BF16)
+
     my_rows = pl.ds(pl.multiple_of(x * REQ, REQ), REQ)
-    merged[my_rows, :] = mine
+    merged[my_rows, :] = here
     row_copies = []
     for o in (2, 1, 3):
         copy = remote(
@@ -516,15 +521,68 @@
         copy.start()
         row_copies.append(copy)
     sends += row_copies
-
-    proj = Wave(
-        mine, rs_own, sib_out, sib_in, rs_out, rs_in, (sib_ssem, sib_rsem, rs_ssem, rs_rsem)
+    stay = Wave(
+        here, rs_own, sib_out, sib_in, rs_out, rs_in, (sib_ssem, sib_rsem, rs_ssem, rs_rsem)
     )
     w_load.wait()
-    proj.opposite(0)
-    proj.same(0)
-    proj.opposite(1)
-    proj.pass_on(0)
+    stay.opposite(0)
+    stay.same(0)
+
+    for copy in far_dn:
+        copy.wait_recv()
+    for copy in s2_far_dn:
+        copy.start()
+    own_up.wait()
+    for copy in near_up:
+        copy.wait_recv()
+    for copy in s2_near_up:
+        copy.start()
+
+    stay.opposite(1)
+    stay.pass_on(0)
+    stay.same(1)
+    stay.opposite(2)
+    stay.pass_on(1)
+    stay.same(2)
+    stay.opposite(3)
+    stay.pass_on(2)
+    stay.same(3)
+    stay.pass_on(3)
+
+    def arrived_at(h):
+        for g in range(SPAN):
+            remote(
+                res.at[0], mig.at[h, pl.ds(8 * g, 8)], mig_ssem.at[g, 0], mig_rsem.at[h, g], sib
+            ).wait_recv()
+
+    mh = iota((128, 32), 0)
+    ml = iota((128, 32), 1)
+
+    def put_rows(recv_row, results, rows):
+        put = ((mh % REQ == recv_row) & (mh // REQ == ml % 4)).astype(BF16)
+        placed = dot(put, results.astype(BF16)).astype(BF16)
+        placed = jnp.concatenate([placed[k * REQ : (k + 1) * REQ] for k in range(HEADS)], axis=1)
+        hit = jnp.where(iota((REQ, 32), 0) == recv_row, 1.0, 0.0)
+        taken = jnp.max(hit, axis=1, keepdims=True) > 0.5
+        return jnp.where(taken, placed, rows), taken
+
+    arrived_at(x)
+    mine, taken = put_rows(recv4[:, 0:32], mig[x], here)
+    moved = jnp.concatenate([mig[x, pl.ds(h, 8, stride=HEADS), :] for h in range(HEADS)], axis=1)
+    moved = jnp.concatenate([moved, jnp.zeros_like(moved)], axis=0).astype(BF16)
+    move = Wave(
+        moved,
+        rs2_own,
+        sib2_out,
+        sib2_in,
+        rs2_out,
+        rs2_in,
+        (sib2_ssem, sib2_rsem, rs2_ssem, rs2_rsem),
+    )
+    move.opposite(0)
+    move.same(0)
+    move.opposite(1)
+    move.pass_on(0)
 
     ad_load.wait()
     slot_col = to_column(
@@ -534,10 +592,22 @@
     c512 = iota((REQ, 512), 1)
     part = dot_nt(mine, adown[...])
     pieces = [jnp.where((c512 // RANK == slot_col) & resident, part, 0.0)]
-    for copy in meta_copies + row_copies + s2_near_dn + s2_far_dn:
-        copy.wait_recv()
-    tcols = [to_column(meta[h][1:2], REQ) for h in range(ROW)]
-    part = dot_nt(merged[...], sdn[...])
+    for copy in meta_copies + row_copies:
+        copy.wait_recv()
+    for o in range(1, 4):
+        arrived_at((x + o) % 4)
+    tiles = [meta[h] for h in range(ROW)]
+    tcols = [to_column(tile[1:2], REQ) for tile in tiles]
+    together = jnp.concatenate(
+        [
+            put_rows(tiles[h][0:1, 0:32], mig[h], merged[h * REQ : (h + 1) * REQ, :])[0]
+            for h in range(ROW)
+        ],
+        axis=0,
+    )
+    for copy in s2_near_dn + s2_far_dn:
+        copy.wait_recv()
+    part = dot_nt(together, sdn[...])
     sections = [
         jnp.where(c512 // RANK_PART == tcols[h], part[h * REQ : (h + 1) * REQ], 0.0)
         for h in range(ROW)
@@ -550,9 +620,9 @@
         copy.wait_recv()
     for copy in s2_far_up:
         copy.start()
-    proj.same(1)
-    proj.opposite(2)
-    proj.pass_on(1)
+    move.same(1)
+    move.opposite(2)
+    move.pass_on(1)
     msg_copy.wait_recv()
     bc[x, z] = (msg[0].astype(F32) + msg_sib[...].astype(F32)).astype(BF16)
     bc_copies = []
@@ -570,11 +640,11 @@
             copy.start()
             bc_copies.append(copy)
     sends += bc_copies
-    proj.same(2)
-    proj.opposite(3)
-    proj.pass_on(2)
-    proj.same(3)
-    proj.pass_on(3)
+    move.same(2)
+    move.opposite(3)
+    move.pass_on(2)
+    move.same(3)
+    move.pass_on(3)
 
     for copy in bc_copies:
         copy.wait_recv()
@@ -620,7 +690,19 @@
         ],
         axis=1,
     ).astype(BF16)
-    acc = dot(spread, aup[...]) + proj.total()
+    acc = dot(spread, aup[...])
+
+    folded = move.total()
+    moved_sum = jnp.concatenate([folded[:8], folded[8:]], axis=1)
+    high = moved_sum.astype(BF16)
+    low = (moved_sum - high.astype(F32)).astype(BF16)
+    both = jnp.concatenate([high, low], axis=0)
+    l16 = iota((REQ, 16), 1) % 8
+    into = jnp.full((REQ, 16), -1, jnp.int32)
+    for j in range(SPAN * CAP):
+        into = jnp.where(l16 == j, recv_s[0, j], into)
+    replaced = dot((into == iota((REQ, 16), 0)).astype(BF16), both)
+    acc = acc + jnp.where(taken, replaced, stay.total())
     for copy in dlt_copies:
         copy.wait_recv()
     out_ref[...] = (
@@ -628,8 +710,13 @@
     ).astype(BF16)
 
     msg_copy.wait_send()
-    for copy in proj.sib_copies + proj.copies + sends:
+    for copy in stay.sib_copies + stay.copies + move.sib_copies + move.copies + sends:
         copy.wait_send()
+    for copy, device in own_results:
+
+        @pl.when(device != r)
+        def _():
+            copy.wait_send()
 
 
 def body(
@@ -680,7 +767,7 @@
             pltpu.VMEM((SPAN, 16, HD), BF16),
             pltpu.VMEM((ROW, 8, 128), jnp.int32),
             pltpu.VMEM((SPAN, 8, HD), F32),
-            pltpu.VMEM((32, HD), F32),
+            pltpu.VMEM((ROW, 32, HD), F32),
             pltpu.VMEM((ROW * REQ, QW), BF16),
             pltpu.VMEM((256, HD), F32),
             pltpu.VMEM((5 * 512, 128), BF16),
@@ -696,6 +783,11 @@
             pltpu.VMEM((4, REQ, OUT), F32),
             pltpu.VMEM((3, REQ, OUT), BF16),
             pltpu.VMEM((3, REQ, OUT), BF16),
+            pltpu.VMEM((4, 16, OUT // 2), BF16),
+            pltpu.VMEM((4, 16, OUT // 2), BF16),
+            pltpu.VMEM((4, 16, OUT // 2), F32),
+            pltpu.VMEM((3, 16, OUT // 2), BF16),
+            pltpu.VMEM((3, 16, OUT // 2), BF16),
             dma((9,)),
             dma((5,)),
             dma((2,)),
@@ -707,13 +799,17 @@
             dma((4,)),
             dma((4,)),
             dma((4,)),
-            dma((4,)),
-            dma((4,)),
+            dma((4, 4)),
+            dma((4, 4)),
             dma((4,)),
             dma((4,)),
             dma((2,)),
             dma((4, 4)),
             dma((4, 4)),
+            dma((4,)),
+            dma((4,)),
+            dma((4,)),
+            dma((4,)),
             dma((4,)),
             dma((4,)),
             dma((4,)),

time: 47.5 us -> 45.8 us (0.964)
  Pallas kernels: 45.9 us -> 44.2 us
    pallas_call x1, Pallas kernels: 45.9 us -> 44.2 us  [body(): pl.pallas_call(kernel, out_shape=jax.ShapeDtypeStruct((REQ, OUT), BF16),...]
where the time goes in v3:
time: 45.8 us; the launch traced here: 45.6 us
  Pallas kernels  44.2 us (97%)
  local copies, waits for them, and re-layouts  1.47 us (3%)
    pallas_call x1, Pallas kernels, body(): pl.pallas_call(kernel, out_shape=jax.ShapeDtypeStruct((REQ, OUT), BF16),...  44.2 us
    unnamed x1, local copies, waits for them, and re-layouts  1.47 us

profile of v3, /device:TPU:1, one launch (start us, length us, event | category | flops | bytes accessed | tf_op | source)
XLA Modules:
  0.0 45.6 jit_solution(769534483997679043)
XLA Ops:
  0.0 44.2 %shard_map.145 = bf16[32,1024]{1,0:T(8,128)(2,1)} custom-call(bf16[32,512]{1,0:T(8,128)(2,1)} %q_hbm.1, bf16[32,128,128]{2,1,0:T(8,128)(2,1)} %k_hbm.1, bf16[32,128,128]{2,1,0:T(8,128)(2,1)} %v_hbm.1, bf16[32,128]{1,0:T(8,128)(2,1)} %nk_hbm.1, bf16[32,128]{1,0:T(8,128)(2,1)} %nv_hbm.1, s32[1,32]{1,0:T(1,128)} %bitcast.10, s32[1,32]{1,0:T(1,128)} %bitcast.11, ...), custom_call_target="tpu_custom_call" | custom-call | tf_op jit(solution)/shard_map/pallas_call | solution.py:744
  44.2 1.5 %copy.17 = bf16[32,1024]{1,0:T(8,128)(2,1)} copy(bf16[32,1024]{1,0:T(8,128)(2,1)} %shard_map.145) | data formatting | bytes 131072

commit v4 on v3

--- a/solution.py
+++ b/solution.py
@@ -395,6 +395,8 @@
         copy.start()
 
     k_load.wait()
+    for copy in far_up:
+        copy.start()
     for copy in q_copies:
         copy.wait_recv()
     head8 = iota((8, HD), 0) // HEADS == 0
@@ -461,8 +463,6 @@
             else:
                 copy.start()
                 sends.append(copy)
-    for copy in far_up:
-        copy.start()
 
     er = iota((256, 128), 0)
     ec = iota((256, 128), 1)
@@ -579,10 +579,6 @@
         rs2_in,
         (sib2_ssem, sib2_rsem, rs2_ssem, rs2_rsem),
     )
-    move.opposite(0)
-    move.same(0)
-    move.opposite(1)
-    move.pass_on(0)
 
     ad_load.wait()
     slot_col = to_column(
@@ -620,9 +616,8 @@
         copy.wait_recv()
     for copy in s2_far_up:
         copy.start()
-    move.same(1)
-    move.opposite(2)
-    move.pass_on(1)
+    move.opposite(0)
+    move.same(0)
     msg_copy.wait_recv()
     bc[x, z] = (msg[0].astype(F32) + msg_sib[...].astype(F32)).astype(BF16)
     bc_copies = []
@@ -640,11 +635,11 @@
             copy.start()
             bc_copies.append(copy)
     sends += bc_copies
-    move.same(2)
-    move.opposite(3)
-    move.pass_on(2)
-    move.same(3)
-    move.pass_on(3)
+    move.pass_on(0)
+    for n in range(1, 4):
+        move.opposite(n)
+        move.same(n)
+        move.pass_on(n)
 
     for copy in bc_copies:
         copy.wait_recv()

time: 45.8 us -> 44.6 us (0.974)
  Pallas kernels: 44.2 us -> 43 us
    pallas_call x1, Pallas kernels: 44.2 us -> 43 us  [body(): pl.pallas_call(kernel, out_shape=jax.ShapeDtypeStruct((REQ, OUT), BF16),...]
where the time goes in v4:
time: 44.6 us; the launch traced here: 44.5 us
  Pallas kernels  43 us (96%)
  local copies, waits for them, and re-layouts  1.47 us (3%)
    pallas_call x1, Pallas kernels, body(): pl.pallas_call(kernel, out_shape=jax.ShapeDtypeStruct((REQ, OUT), BF16),...  43 us
    unnamed x1, local copies, waits for them, and re-layouts  1.47 us

profile of v4, /device:TPU:1, one launch (start us, length us, event | category | flops | bytes accessed | tf_op | source)
XLA Modules:
  0.0 44.5 jit_solution(8997832145332526320)
XLA Ops:
  0.0 43.0 %shard_map.145 = bf16[32,1024]{1,0:T(8,128)(2,1)} custom-call(bf16[32,512]{1,0:T(8,128)(2,1)} %q_hbm.1, bf16[32,128,128]{2,1,0:T(8,128)(2,1)} %k_hbm.1, bf16[32,128,128]{2,1,0:T(8,128)(2,1)} %v_hbm.1, bf16[32,128]{1,0:T(8,128)(2,1)} %nk_hbm.1, bf16[32,128]{1,0:T(8,128)(2,1)} %nv_hbm.1, s32[1,32]{1,0:T(1,128)} %bitcast.10, s32[1,32]{1,0:T(1,128)} %bitcast.11, ...), custom_call_target="tpu_custom_call" | custom-call | tf_op jit(solution)/shard_map/pallas_call | solution.py:739
  43.0 1.5 %copy.17 = bf16[32,1024]{1,0:T(8,128)(2,1)} copy(bf16[32,1024]{1,0:T(8,128)(2,1)} %shard_map.145) | data formatting | bytes 131072

commit v5 on v4

--- a/solution.py
+++ b/solution.py
@@ -544,10 +544,7 @@
     stay.opposite(2)
     stay.pass_on(1)
     stay.same(2)
-    stay.opposite(3)
     stay.pass_on(2)
-    stay.same(3)
-    stay.pass_on(3)
 
     def arrived_at(h):
         for g in range(SPAN):
@@ -636,6 +633,9 @@
             bc_copies.append(copy)
     sends += bc_copies
     move.pass_on(0)
+    stay.opposite(3)
+    stay.same(3)
+    stay.pass_on(3)
     for n in range(1, 4):
         move.opposite(n)
         move.same(n)

time: 44.6 us -> 44.3 us (level)
  no operation moved by 1% of the time
where the time goes in v5:
time: 44.3 us; the launch traced here: 44.2 us
  Pallas kernels  42.7 us (96%)
  local copies, waits for them, and re-layouts  1.47 us (3%)
    pallas_call x1, Pallas kernels, body(): pl.pallas_call(kernel, out_shape=jax.ShapeDtypeStruct((REQ, OUT), BF16),...  42.7 us
    unnamed x1, local copies, waits for them, and re-layouts  1.47 us

profile of v5, /device:TPU:1, one launch (start us, length us, event | category | flops | bytes accessed | tf_op | source)
XLA Modules:
  0.0 44.2 jit_solution(10430851175638783849)
XLA Ops:
  0.0 42.7 %shard_map.145 = bf16[32,1024]{1,0:T(8,128)(2,1)} custom-call(bf16[32,512]{1,0:T(8,128)(2,1)} %q_hbm.1, bf16[32,128,128]{2,1,0:T(8,128)(2,1)} %k_hbm.1, bf16[32,128,128]{2,1,0:T(8,128)(2,1)} %v_hbm.1, bf16[32,128]{1,0:T(8,128)(2,1)} %nk_hbm.1, bf16[32,128]{1,0:T(8,128)(2,1)} %nv_hbm.1, s32[1,32]{1,0:T(1,128)} %bitcast.10, s32[1,32]{1,0:T(1,128)} %bitcast.11, ...), custom_call_target="tpu_custom_call" | custom-call | tf_op jit(solution)/shard_map/pallas_call | solution.py:739
  42.7 1.5 %copy.17 = bf16[32,1024]{1,0:T(8,128)(2,1)} copy(bf16[32,1024]{1,0:T(8,128)(2,1)} %shard_map.145) | data formatting | bytes 131072
